TPU v7x, 1024 devices: a whole 8x8x8 slice. The times are simulated.
1024 devices in a mesh: pipe: 16 (over y, core), expert: 16 (over x_lo, z), dp: 4 (over x_hi).
Axes of the slice: x: 8 (x_hi: 4, x_lo: 2; x = x_hi * 2 + x_lo), y: 8, z: 8, core: 2. Of those that a mesh axis runs over, the one named last changes fastest.
Arguments:
- tokens: bfloat16 [16, 2048, 4096], P('pipe', 'expert'), may hold values from -6 to 6
- modality: int32 [16, 2048], P('pipe', 'expert'), may hold values 0 or 1
- routes: int32 [16, 2048, 1], P('pipe', 'expert'), may hold values from 0 to 3; in each aligned block of 128 rows (0 to 127, 128 to 255, ..., all dimensions but the last counted through in order) at most 64 rows name the same one
- norm_gain: float32 [4096], replicated, may hold values from 0.5 to 1.5
- router: bfloat16 [2, 4096, 4], replicated, may hold values from -0.09375 to 0.09375
- gate_weight: bfloat16 [16, 4096, 7168], P('pipe', 'dp', 'expert'), may hold values from -0.09375 to 0.09375
- down_weight: bfloat16 [16, 7168, 4096], P('pipe', 'expert', 'dp'), may hold values from -0.125 to 0.125
Outputs:
- section_output: bfloat16 [16, 2048, 4096], P('pipe', 'expert', 'dp')
Inputs may be any that keep to these rules, and one draw needn't show every extreme that they name: `routes`: among the rows of one device (aligned blocks of 128 rows of a section) no expert is named more than 64 times, and in every draw some device names one expert exactly 64 times.
All inputs are finite; a program needn't handle non-finite values. No bound on the sum of `modality` on one device may be relied on, other than what follows from the above.
Results may differ from a plain program's by a relative error of at most 0.0036.
Values may be sent and summed in bfloat16 or wider, within the bound.
A program may use at most 32 MiB of HBM per device.

v0:
```python
import jax
import jax.numpy as jnp
from jax import lax
from jax.sharding import PartitionSpec as P

epsilon = 1e-06


def shifted(value, axis, steps):
    count = lax.axis_size(axis)
    pairs = [(source, (source + steps) % count) for source in range(count)]
    return lax.ppermute(value, axis, pairs)


def local(tokens, modality, routes, norm_gain, router, gate_weight, down_weight):
    arriving = shifted(tokens, "pipe", 1)
    inputs = arriving[0]
    tok_count = inputs.shape[0]
    width = inputs.shape[1]
    stream = inputs.astype(jnp.float32)
    scale = lax.rsqrt(jnp.mean(stream * stream, axis=-1, keepdims=True) + epsilon)
    normed = (stream * scale * norm_gain).astype(jnp.bfloat16)
    logits = jnp.einsum("td,mde->mte", normed, router, preferred_element_type=jnp.float32)
    token_kind = modality[0]
    route_flat = routes[0, :, 0]
    expert_count = router.shape[2]
    capacity = 2 * tok_count // expert_count
    chosen = jnp.where(token_kind[:, None] == 1, logits[1], logits[0])
    matches = route_flat[:, None] == jnp.arange(expert_count, dtype=jnp.int32)[None, :]
    route_logit = jnp.sum(jnp.where(matches, chosen, 0.0), axis=1)
    gate_value = jax.nn.sigmoid(route_logit)
    hits = matches.astype(jnp.int32)
    earlier = jnp.cumsum(hits, axis=0) - hits
    own_rank = jnp.sum(jnp.where(matches, earlier, 0), axis=1)
    slot_index = route_flat * capacity + own_rank
    placer = (
        jnp.arange(expert_count * capacity, dtype=jnp.int32)[:, None] == slot_index[None, :]
    ).astype(jnp.bfloat16)
    dp_size = lax.axis_size("dp")
    width_part = width // dp_size
    own_columns = lax.dynamic_slice_in_dim(normed, lax.axis_index("dp") * width_part, width_part, 1)
    packed = jnp.dot(placer, own_columns, preferred_element_type=jnp.float32).astype(jnp.bfloat16)
    owners = lax.axis_size("expert")
    group_size = owners // expert_count
    packed = packed.reshape(expert_count, 1, capacity, width_part)
    packed = jnp.broadcast_to(packed, (expert_count, group_size, capacity, width_part))
    packed = packed.reshape(owners, capacity, width_part)
    local_gate = gate_weight[0]
    local_down = down_weight[0]
    received = lax.all_to_all(packed, "expert", split_axis=0, concat_axis=0, tiled=True)
    source_count = received.shape[0]
    slot_count = received.shape[1]
    flattened = received.reshape(-1, width_part)
    gate_terms = jnp.dot(flattened, local_gate, preferred_element_type=jnp.float32)
    gate_full = lax.psum(gate_terms, "dp")
    hidden = jax.nn.silu(gate_full).astype(jnp.bfloat16)
    out_term = jnp.dot(hidden, local_down, preferred_element_type=jnp.float32).astype(jnp.bfloat16)
    out_term = out_term.reshape(source_count, slot_count, width_part)
    returned = lax.all_to_all(out_term, "expert", split_axis=0, concat_axis=0, tiled=True)
    grouped = returned.reshape(expert_count, group_size, capacity, width_part).astype(jnp.float32)
    summed = (
        jnp.sum(grouped, axis=1).astype(jnp.bfloat16).reshape(expert_count * capacity, width_part)
    )
    expert_out = jnp.einsum("st,sd->td", placer, summed, preferred_element_type=jnp.float32)
    residual = lax.dynamic_slice_in_dim(stream, lax.axis_index("dp") * width_part, width_part, 1)
    result = residual + gate_value[:, None] * expert_out
    return result.astype(jnp.bfloat16)[None]


def solution(mesh):
    placed = (
        P("pipe", "expert", None),
        P("pipe", "expert"),
        P("pipe", "expert", None),
        P(),
        P(),
        P("pipe", "dp", "expert"),
        P("pipe", "expert", "dp"),
    )
    return jax.shard_map(
        local, mesh=mesh, in_specs=placed, out_specs=P("pipe", "expert", "dp"), check_vma=False
    )
```

profile of v0, /device:TPU:6, one launch (start us, length us, event | category | flops | bytes accessed | tf_op | source)
XLA Modules:
  0.0 268.1 jit_solution(2248645506823691459)
XLA Ops:
  6.5 0.0 copy-start
  6.5 0.0 all-reduce.2.cloned.1.call-start
  6.5 0.0 collective-permute-start
  6.5 0.7 fusion.16
  7.3 0.1 copy.8
  7.4 0.2 reduce_window_sum.11
  7.6 0.1 copy.9
  7.6 0.7 select_reduce_fusion
  8.3 0.7 multiply_add_fusion
  9.0 14.0 %collective-permute-done = bf16[1,128,4096]{2,1,0:T(8,128)(2,1)S(1)} collective-permute-done((bf16[1,128,4096]{2,1,0:T(8,128)(2,1)}, bf16[1,128,4096]{2,1,0:T(8,128)(2,1)S(1)}, u32[]{:S(2)}, u32[]{:S(2)}) %collective-permute-start) | collective-permute-done | bytes 1048608 | tf_op jit(solution)/shard_map/ppermute | solution.py:12
  22.9 0.3 fusion
  23.2 1.0 fusion.2
  24.3 0.3 convolution_convert_fusion.1
  24.6 0.3 broadcast_in_dim.36
  24.9 0.0 copy-start.3
  24.9 65.1 %all_to_all.10 = bf16[16,64,1024]{2,1,0:T(8,128)(2,1)S(1)} all-to-all(bf16[16,64,1024]{2,1,0:T(8,128)(2,1)S(1)} %bitcast.55), channel_id=1, replica_groups=mesh['pipe'=16,'expert'=16,'dp'=4] {'expert'}, dimensions={0} | all-to-all | bytes 4194304 | tf_op jit(solution)/shard_map/all_to_all | solution.py:50
  90.0 0.0 copy-done.3
  90.0 2.4 fusion.5
  92.4 0.0 all-reduce.2.cloned.1.call-update
  92.5 96.5 %all-reduce.2.cloned.1.call-done = f32[1024,448]{0,1:T(8,128)} async-done(((f32[1024,448]{0,1:T(8,128)}), f32[1024,448]{0,1:T(8,128)}) %all-reduce.2.cloned.1.call-update) | async-done | bytes 1835024 | tf_op jit(solution)/shard_map/psum | solution.py:55
  188.9 0.0 copy-done
  189.0 4.2 %convolution_convert_fusion = bf16[1024,1024]{1,0:T(8,128)(2,1)} fusion(f32[1024,448]{0,1:T(8,128)} %all-reduce.2.cloned.1.call-done, bf16[1,448,1024]{2,1,0:T(8,128)(2,1)S(1)} %copy-done), kind=kOutput, calls=%fused_computation.6 | convolution fusion | flops 942866432 | bytes 4849664 | tf_op jit(solution)/shard_map/dot_general | solution.py:57
  193.1 0.0 copy-start.4
  193.1 11.3 %all-to-all-start.1 = ((bf16[16,64,1024]{2,1,0:T(8,128)(2,1)}), bf16[16,64,1024]{2,1,0:T(8,128)(2,1)}, u32[]{:S(2)}, u32[]{:S(2)}) async-start(bf16[16,64,1024]{2,1,0:T(8,128)(2,1)} %bitcast.58), calls=%async_computation.1 | async-start | bytes 4194304 | tf_op jit(solution)/shard_map/all_to_all | solution.py:59
  204.5 0.0 copy-done.4
  204.5 0.0 copy-start.1
  204.5 0.0 copy-start.2
  204.5 1.5 convert_element_type.27
  206.0 0.0 copy-done.1
  206.0 0.4 convolution_bitcast_fusion
  206.4 0.0 copy-done.2
  206.5 50.7 %all-to-all-done.1 = bf16[16,64,1024]{2,1,0:T(8,128)(2,1)} async-done(((bf16[16,64,1024]{2,1,0:T(8,128)(2,1)}), bf16[16,64,1024]{2,1,0:T(8,128)(2,1)}, u32[]{:S(2)}, u32[]{:S(2)}) %all-to-all-start.1) | async-done | bytes 2097184 | tf_op jit(solution)/shard_map/all_to_all | solution.py:59
  257.2 2.0 bitcast_reduce_fusion
  259.2 2.0 fusion.9
  (4 shorter events, 0.1 us)
Async XLA Ops:
  6.5 182.4 %copy-start = (bf16[1,448,1024]{2,1,0:T(8,128)(2,1)S(1)}, bf16[1,448,1024]{2,1,0:T(8,128)(2,1)}, u32[]{:S(2)}) copy-start(bf16[1,448,1024]{2,1,0:T(8,128)(2,1)} %param.13) | copy-start | bytes 2752516
  6.5 182.4 %all-reduce.2.cloned.1.call-start = ((), (), s32[]{:S(2)}) async-start(), calls=%async_computation.2 | async-start | bytes 3670016 | tf_op jit(solution)/shard_map/psum | solution.py:55
  6.5 16.4 %collective-permute-start = (bf16[1,128,4096]{2,1,0:T(8,128)(2,1)}, bf16[1,128,4096]{2,1,0:T(8,128)(2,1)S(1)}, u32[]{:S(2)}, u32[]{:S(2)}) collective-permute-start(bf16[1,128,4096]{2,1,0:T(8,128)(2,1)} %param.7), channel_id=1, source_target_pairs={{0,64},{64,128},{128,192},{192,256},{256,320},{320,384},{384,448},... | collective-permute-start | bytes 3145736 | tf_op jit(solution)/shard_map/ppermute | solution.py:12
  24.9 65.2 %copy-start.3 = (bf16[1,1024,448]{1,2,0:T(8,128)(2,1)S(1)}, bf16[1,1024,448]{1,2,0:T(8,128)(2,1)}, u32[]{:S(2)}) copy-start(bf16[1,1024,448]{1,2,0:T(8,128)(2,1)} %param.12) | copy-start | bytes 2752516
  193.1 11.3 %copy-start.4 = (s32[1,128]{1,0:T(1,128)S(1)}, s32[1,128]{1,0:T(1,128)}, u32[]{:S(2)}) copy-start(s32[1,128]{1,0:T(1,128)} %param.8) | copy-start | bytes 1540
  193.1 64.1 %all-to-all-start.1 = ((bf16[16,64,1024]{2,1,0:T(8,128)(2,1)}), bf16[16,64,1024]{2,1,0:T(8,128)(2,1)}, u32[]{:S(2)}, u32[]{:S(2)}) async-start(bf16[16,64,1024]{2,1,0:T(8,128)(2,1)} %bitcast.58), calls=%async_computation.1 | async-start | bytes 4194304 | tf_op jit(solution)/shard_map/all_to_all | solution.py:59
  204.5 1.6 copy-start.1
  204.5 1.9 copy-start.2
Sparse Core Ops, SparseCore 0:
  92.6 96.3 all-reduce.1
where the time goes:
time: 268 us
  waiting for transfers between devices  161 us (60%)
  blocking collectives  65.1 us (24%)
  between operations  13.5 us (5%)
  starting transfers between devices  11.3 us (4%)
  matrix products  9.31 us (3%)
  other arithmetic  7.18 us (3%)
    psum x1, waiting for transfers between devices, local(): gate_full = lax.psum(gate_terms, 'dp')  96.5 us
    all_to_all x1, blocking collectives, local(): lax.all_to_all(packed, 'expert', split_axis=0, concat_axis=0, tiled=True)  65.1 us
    all_to_all x1, waiting for transfers between devices, local(): lax.all_to_all(out_term, 'expert', split_axis=0, concat_axis=0, tiled=True)  50.7 us
    ppermute x1, waiting for transfers between devices, shifted(): return lax.ppermute(value, axis, pairs)  14 us
    all_to_all x1, starting transfers between devices, local(): lax.all_to_all(out_term, 'expert', split_axis=0, concat_axis=0, tiled=True)  11.3 us
  transfers between devices with their start and end apart: 3, of which 3 were waited for; matrix products, arithmetic and copies ran while one was open for 2% of the time, Pallas kernels for 0%

commit v1 on v0

v1 whole, which is shorter than its diff:
```python
import functools

import jax
import jax.numpy as jnp
from jax import lax
from jax.experimental import pallas as pl
from jax.experimental.pallas import tpu as pltpu
from jax.sharding import PartitionSpec as P

MESH = pl.DeviceIdType.MESH
epsilon = 1e-06
Z = 8
STEPS = 8


def kernel(
    n_pipe, n_dp,
    tokens, modality, routes, gain, router, gate_hbm, down_hbm,
    out,
    tok_v, normed_v, gate_v, down_v, arrived, stat_tx, stat_rx, placer, unplacer, chosen,
    packed, recv, rs_tx, rs_rx, own_sum, hid, term, ret_far, ret_near, fin,
    local_sem, pipe_send, pipe_recv, first_send, forward_send, dispatch_recv,
    sum_send, sum_recv, hid_send, hid_recv, ret_send, far_recv, near_recv, fin_recv,
):
    tok = tok_v.shape[0]
    cap = recv.shape[1] // 2
    part = recv.shape[2]
    piece = rs_rx.shape[2]
    s, j, d = lax.axis_index("pipe"), lax.axis_index("expert"), lax.axis_index("dp")
    xl, z = j // Z, j % Z
    g, p = z // 4, z % 4
    mid = ((p + 1) // 2) % 2
    nd = 2 * (p // 2) - 1
    near, far = (z + nd + Z) % Z, (z - nd + Z) % Z
    across = (z + nd * (1 + mid) + Z) % Z
    second = (z + 2 * nd + Z) % Z
    beside = (z + nd * (1 - 2 * mid) + Z) % Z
    other = 1 - xl
    is_mid = mid == 1
    is_end = mid == 0

    def at(x, zz):
        return (s, x * Z + zz, d)

    def send(src, dst, send_sem, recv_sem, device):
        return pltpu.make_async_remote_copy(
            src_ref=src, dst_ref=dst, send_sem=send_sem, recv_sem=recv_sem,
            device_id=device, device_id_type=MESH,
        )

    def rows(ref, zz, x):
        return ref.at[zz, pl.ds(pl.multiple_of(x * cap, cap), cap)]

    tok_copy = pltpu.make_async_copy(tokens, tok_v, local_sem.at[0])
    gate_copy = pltpu.make_async_copy(gate_hbm, gate_v, local_sem.at[1])
    down_copy = pltpu.make_async_copy(down_hbm, down_v, local_sem.at[2])
    tok_copy.start()

    barrier = pltpu.get_barrier_semaphore()
    partners = [
        ((s + 1) % n_pipe, j, d),
        ((s + n_pipe - 1) % n_pipe, j, d),
        at(other, z), at(xl, near), at(xl, far), at(xl, second), at(other, second), at(other, beside),
    ] + [(s, j, (d + k) % n_dp) for k in range(1, n_dp)]
    for device in partners:
        pl.semaphore_signal(barrier, inc=1, device_id=device, device_id_type=MESH)
    gate_copy.start()
    down_copy.start()

    route_row = routes[...]
    hits = (lax.broadcasted_iota(jnp.int32, (8, tok), 0) == route_row).astype(jnp.float32)
    before = (
        lax.broadcasted_iota(jnp.int32, (tok, tok), 0) < lax.broadcasted_iota(jnp.int32, (tok, tok), 1)
    ).astype(jnp.bfloat16)
    earlier = jnp.dot(hits.astype(jnp.bfloat16), before, preferred_element_type=jnp.float32)
    rank = jnp.sum(hits * earlier, axis=0, keepdims=True)
    slot_row = route_row.astype(jnp.float32) * cap + rank
    slots = lax.broadcasted_iota(jnp.int32, (4 * cap, tok), 0).astype(jnp.float32)
    placer[...] = (slots == slot_row).astype(jnp.bfloat16)
    slot_col = jnp.transpose(jnp.broadcast_to(slot_row, (tok, tok)))[:, 0:1]
    slots = lax.broadcasted_iota(jnp.int32, (tok, 4 * cap), 1).astype(jnp.float32)
    unplacer[...] = (slots == slot_col).astype(jnp.bfloat16)
    pick_row = (modality[...] * 4 + route_row).astype(jnp.float32)
    pick_col = jnp.transpose(jnp.broadcast_to(pick_row, (tok, tok)))[:, 0:1]
    lanes = lax.broadcasted_iota(jnp.int32, (tok, 128), 1).astype(jnp.float32)
    chosen[...] = (lanes == pick_col).astype(jnp.float32)

    pl.semaphore_wait(barrier, len(partners))

    following = ((s + 1) % n_pipe, j, d)
    own_columns = pl.ds(pl.multiple_of(d * part, part), part)
    raw_copy = send(tokens.at[:, own_columns], arrived, pipe_send.at[0], pipe_recv.at[0], following)
    raw_copy.start()

    stat_tx[...] = jnp.zeros_like(stat_tx)
    tok_copy.wait()

    def norm_rows(i, carry):
        block = pl.ds(pl.multiple_of(i * 16, 16), 16)
        x = tok_v[block, :].astype(jnp.float32)
        scale = lax.rsqrt(jnp.mean(x * x, axis=-1, keepdims=True) + epsilon)
        normed_v[block, :] = (x * scale * gain[...]).astype(jnp.bfloat16)
        stat_tx[block, 8:9] = scale
        return carry

    lax.fori_loop(0, tok // 16, norm_rows, 0)
    for kind in range(2):
        stat_tx[:, 4 * kind : 4 * kind + 4] = lax.dot_general(
            normed_v[...], router[kind], (((1,), (1,)), ((), ())), preferred_element_type=jnp.float32
        )
    stat_copy = send(stat_tx, stat_rx, pipe_send.at[1], pipe_recv.at[1], following)
    stat_copy.start()
    raw_copy.wait_recv()
    stat_copy.wait_recv()

    scale = stat_rx[:, 8:9]
    normed = (arrived[...].astype(jnp.float32) * scale * gain[:, own_columns]).astype(jnp.bfloat16)

    def pack(x, group):
        spot = pl.ds(pl.multiple_of((2 * x + group) * cap, cap), cap)
        return jnp.dot(placer[spot, :], normed, preferred_element_type=jnp.float32).astype(jnp.bfloat16)

    packed[0] = pack(other, g)
    cross = send(packed.at[0], rows(recv, z, xl), first_send.at[0], dispatch_recv.at[z, xl], at(other, z))
    cross.start()
    recv[z, pl.ds(pl.multiple_of(xl * cap, cap), cap), :] = pack(xl, g)
    own_far = send(rows(recv, z, xl), rows(recv, z, xl), first_send.at[1], dispatch_recv.at[z, xl], at(xl, far))
    own_near = send(rows(recv, z, xl), rows(recv, z, xl), first_send.at[2], dispatch_recv.at[z, xl], at(xl, near))
    own_far.start()

    @pl.when(is_mid)
    def _():
        own_near.start()

    packed[1] = pack(xl, 1 - g)
    ext_own = send(packed.at[1], rows(recv, z, xl), first_send.at[3], dispatch_recv.at[z, xl], at(xl, across))
    ext_own.start()
    packed[2] = pack(other, 1 - g)
    ext_other = send(packed.at[2], rows(recv, z, xl), first_send.at[4], dispatch_recv.at[z, xl], at(other, across))
    ext_other.start()

    relay_far = send(rows(recv, z, other), rows(recv, z, other), first_send.at[5], dispatch_recv.at[z, other], at(xl, far))
    relay_near = send(rows(recv, z, other), rows(recv, z, other), first_send.at[6], dispatch_recv.at[z, other], at(xl, near))
    relay_far.wait_recv()
    relay_far.start()

    @pl.when(is_mid)
    def _():
        relay_near.start()

    gate_copy.wait()
    down_copy.wait()

    def source(t):
        late = (1 - mid) * (t // 5)
        usual = (t % 2) * ((t + 1) // 2) - (1 - t % 2) * (t // 2)
        offset = usual * (1 - late) + late * (2 - t)
        return (z + nd * offset + 2 * Z) % Z

    def forward(t, zz, x):
        to_near = mid * (1 - (t % 2) * (1 - t // 7))
        target = (z + nd * (2 * to_near - 1) + Z) % Z
        return send(rows(recv, zz, x), rows(recv, zz, x), forward_send.at[t, x], dispatch_recv.at[zz, x], at(xl, target))

    def forwards(t):
        return (t >= 1) & (is_mid | (t == 1) | (t == 3))

    def sum_copy(t, k):
        q = (d + k) % n_dp
        return send(
            rs_tx.at[t, pl.ds(pl.multiple_of(q * piece, piece), piece)], rs_rx.at[t, k - 1],
            sum_send.at[t, k - 1], sum_recv.at[t, k - 1], (s, j, q),
        )

    def hid_copy(t, k):
        own = hid.at[t, pl.ds(pl.multiple_of(d * piece, piece), piece)]
        return send(own, own, hid_send.at[t, k - 1], hid_recv.at[t, k - 1], (s, j, (d + k) % n_dp))

    def leaf_copy(zz, x):
        return send(rows(ret_near, zz, x), rows(ret_near, zz, x), ret_send.at[zz, x], near_recv.at[zz, x], at(xl, far))

    def up_copy(zz, x):
        return send(rows(ret_near, zz, x), rows(ret_far, zz, x), ret_send.at[zz, x], far_recv.at[zz, x], at(xl, far))

    def down_chain(zz, x):
        return send(rows(ret_far, zz, x), rows(ret_far, zz, x), ret_send.at[zz, x], far_recv.at[zz, x], at(xl, near))

    own_expert = 2 * xl + g

    def home_copy(zz, x):
        return send(rows(ret_far, zz, x), fin.at[own_expert], ret_send.at[zz, x], fin_recv.at[own_expert], at(x, zz))

    def each_step(i, carry):
        @pl.when(i <= 7)
        def _():
            zz = source(i)
            for x in (xl, other):
                @pl.when(i >= 1)
                def _():
                    forward(i, zz, x).wait_recv()

                @pl.when(forwards(i))
                def _():
                    forward(i, zz, x).start()

            terms = lax.dot_general(
                recv[zz], gate_v[...], (((1,), (1,)), ((), ())), preferred_element_type=jnp.float32
            )
            own_sum[i % 2] = terms
            rs_tx[i] = terms.astype(jnp.bfloat16)
            for k in range(1, n_dp):
                sum_copy(i, k).start()

        @pl.when((i >= 1) & (i <= 8))
        def _():
            t = i - 1
            for k in range(1, n_dp):
                sum_copy(t, k).wait_recv()
            mine = pl.ds(pl.multiple_of(d * piece, piece), piece)
            total = own_sum[t % 2, mine, :]
            for k in range(1, n_dp):
                total = total + rs_rx[t, k - 1].astype(jnp.float32)
            hid[t, mine, :] = (total / (1.0 + jnp.exp(-total))).astype(jnp.bfloat16)
            for k in range(1, n_dp):
                hid_copy(t, k).start()

        @pl.when((i >= 2) & (i <= 9))
        def _():
            t = i - 2
            zz = source(t)
            for k in range(1, n_dp):
                hid_copy(t, k).wait_recv()
            term[zz] = jnp.dot(hid[t], down_v[...], preferred_element_type=jnp.float32)

            @pl.when(is_end & ((t == 2) | (t >= 4)))
            def _():
                ret_near[zz] = term[zz].astype(jnp.bfloat16)
                for x in range(2):
                    leaf_copy(zz, x).start()

        @pl.when(is_mid & (i >= 7) & (i <= 10))
        def _():
            zz = (z - nd * (i - 6) + Z) % Z
            for x in range(2):
                leaf_copy(zz, x).wait_recv()
                span = slice(x * cap, (x + 1) * cap)
                ret_near[zz, span] = (term[zz, span] + ret_near[zz, span].astype(jnp.float32)).astype(jnp.bfloat16)
                up_copy(zz, x).start()

        @pl.when(is_mid & (i >= 9) & (i <= 11))
        def _():
            zz = (z + nd * (i - 8) + Z) % Z
            for x in range(2):
                down_chain(zz, x).wait_recv()
                span = slice(x * cap, (x + 1) * cap)
                ret_far[zz, span] = (term[zz, span] + ret_far[zz, span].astype(jnp.float32)).astype(jnp.bfloat16)
                down_chain(zz, x).start()

        @pl.when((is_mid & (i == 8)) | (is_end & (i == 10)))
        def _():
            for x in (other, xl):
                span = pl.ds(pl.multiple_of(x * cap, cap), cap)
                up_copy(z, x).wait_recv()
                ret_far[z, span, :] = (term[z, span, :] + ret_far[z, span, :].astype(jnp.float32)).astype(jnp.bfloat16)

                @pl.when(is_mid)
                def _():
                    leaf_copy(z, x).wait_recv()
                    ret_far[z, span, :] = (
                        ret_far[z, span, :].astype(jnp.float32) + ret_near[z, span, :].astype(jnp.float32)
                    ).astype(jnp.bfloat16)

                if x is other:
                    home_copy(z, other).start()
            fin[own_expert] = ret_far[z, pl.ds(pl.multiple_of(xl * cap, cap), cap), :]

        @pl.when(is_end & (i >= 11))
        def _():
            zz = (z + nd * (i - 10) + Z) % Z
            for x in range(2):
                up_copy(zz, x).wait_recv()
                span = slice(x * cap, (x + 1) * cap)
                ret_far[zz, span] = (term[zz, span] + ret_far[zz, span].astype(jnp.float32)).astype(jnp.bfloat16)
                home_copy(zz, x).start()

        return carry

    lax.fori_loop(0, 13, each_step, 0)

    for x, group in ((other, g), (xl, 1 - g), (other, 1 - g)):
        e = 2 * x + group
        send(fin.at[e], fin.at[e], ret_send.at[0, 0], fin_recv.at[e], at(other, z)).wait_recv()

    gate_value = 1.0 / (1.0 + jnp.exp(-jnp.sum(chosen[...] * stat_rx[...], axis=1, keepdims=True)))
    expert_out = jnp.dot(
        unplacer[...], fin[...].reshape(4 * cap, part), preferred_element_type=jnp.float32
    )
    out[...] = (arrived[...].astype(jnp.float32) + gate_value * expert_out).astype(jnp.bfloat16)

    raw_copy.wait_send()
    stat_copy.wait_send()
    for copy in (cross, own_far, ext_own, ext_other, relay_far):
        copy.wait_send()

    @pl.when(is_mid)
    def _():
        own_near.wait_send()
        relay_near.wait_send()

    def sent(t, carry):
        zz = source(t)

        @pl.when(forwards(t))
        def _():
            for x in range(2):
                forward(t, zz, x).wait_send()

        for k in range(1, n_dp):
            sum_copy(t, k).wait_send()
            hid_copy(t, k).wait_send()

        @pl.when(t >= 1)
        def _():
            for x in range(2):
                leaf_copy(zz, x).wait_send()

        return carry

    lax.fori_loop(0, STEPS, sent, 0)
    home_copy(z, other).wait_send()


def local(tokens, modality, routes, norm_gain, router, gate_weight, down_weight):
    tok, width = tokens.shape[1:]
    n_pipe, n_dp = lax.axis_size("pipe"), lax.axis_size("dp")
    part = width // n_dp
    cap = 2 * tok // router.shape[2]
    hidden = gate_weight.shape[2]
    piece = 2 * cap // n_dp
    bf16, f32 = jnp.bfloat16, jnp.float32
    vmem = pl.BlockSpec(memory_space=pltpu.VMEM)
    anywhere = pl.BlockSpec(memory_space=pl.ANY)
    dma = pltpu.SemaphoreType.DMA
    result = pl.pallas_call(
        functools.partial(kernel, n_pipe, n_dp),
        out_shape=jax.ShapeDtypeStruct((tok, part), bf16),
        in_specs=[anywhere, vmem, vmem, vmem, vmem, anywhere, anywhere],
        out_specs=vmem,
        scratch_shapes=[
            pltpu.VMEM((tok, width), bf16),
            pltpu.VMEM((tok, width), bf16),
            pltpu.VMEM((hidden, part), bf16),
            pltpu.VMEM((hidden, part), bf16),
            pltpu.VMEM((tok, part), bf16),
            pltpu.VMEM((tok, 128), f32),
            pltpu.VMEM((tok, 128), f32),
            pltpu.VMEM((4 * cap, tok), bf16),
            pltpu.VMEM((tok, 4 * cap), bf16),
            pltpu.VMEM((tok, 128), f32),
            pltpu.VMEM((3, cap, part), bf16),
            pltpu.VMEM((STEPS, 2 * cap, part), bf16),
            pltpu.VMEM((STEPS, 2 * cap, hidden), bf16),
            pltpu.VMEM((STEPS, n_dp - 1, piece, hidden), bf16),
            pltpu.VMEM((2, 2 * cap, hidden), f32),
            pltpu.VMEM((STEPS, 2 * cap, hidden), bf16),
            pltpu.VMEM((STEPS, 2 * cap, part), f32),
            pltpu.VMEM((STEPS, 2 * cap, part), bf16),
            pltpu.VMEM((STEPS, 2 * cap, part), bf16),
            pltpu.VMEM((4, cap, part), bf16),
            dma((3,)),
            dma((2,)),
            dma((2,)),
            dma((7,)),
            dma((STEPS, 2)),
            dma((STEPS, 2)),
            dma((STEPS, n_dp - 1)),
            dma((STEPS, n_dp - 1)),
            dma((STEPS, n_dp - 1)),
            dma((STEPS, n_dp - 1)),
            dma((STEPS, 2)),
            dma((STEPS, 2)),
            dma((STEPS, 2)),
            dma((4,)),
        ],
        compiler_params=pltpu.CompilerParams(
            collective_id=0, has_side_effects=True, vmem_limit_bytes=48 * 1024 * 1024
        ),
    )(
        tokens[0],
        modality,
        routes.reshape(1, tok),
        norm_gain.reshape(1, width),
        jnp.transpose(router, (0, 2, 1)),
        jnp.transpose(gate_weight[0]),
        down_weight[0],
    )
    return result[None]


def solution(mesh):
    placed = (
        P("pipe", "expert", None),
        P("pipe", "expert"),
        P("pipe", "expert", None),
        P(),
        P(),
        P("pipe", "dp", "expert"),
        P("pipe", "expert", "dp"),
    )
    return jax.shard_map(
        local, mesh=mesh, in_specs=placed, out_specs=P("pipe", "expert", "dp"), check_vma=False
    )
```

time: 268 us -> 126 us (0.47)
  the two profiles are of different devices: /device:TPU:6 before, /device:TPU:64 now
where the time goes in v1:
time: 126 us
  Pallas kernels  119 us (94%)
  local copies, waits for them, and re-layouts  6.51 us (5%)
    pallas_call x1, Pallas kernels, local(): pl.pallas_call(functools.partial(kernel, n_pipe, n_dp), out_shape=jax.Sha...  119 us
    unnamed x15, local copies, waits for them, and re-layouts  6.51 us

profile of v1, /device:TPU:64, one launch (start us, length us, event | category | flops | bytes accessed | tf_op | source)
XLA Modules:
  0.0 125.9 jit_solution(6422311200155319484)
XLA Ops:
  0.0 0.0 copy-start.5
  0.0 0.0 copy-start.6
  0.0 0.7 copy-done.5
  0.7 0.0 copy-done.6
  0.7 0.0 copy-start
  0.7 1.2 copy-done
  1.9 0.0 copy-start.1
  1.9 1.2 copy-done.1
  3.1 0.0 copy-start.2
  3.1 1.2 copy-done.2
  4.3 0.0 copy-start.3
  4.3 0.8 copy-done.3
  5.1 0.0 copy-start.4
  5.1 0.7 copy-done.4
  5.8 119.4 %shard_map.73 = bf16[128,1024]{1,0:T(8,128)(2,1)S(1)} custom-call(bf16[128,4096]{1,0:T(8,128)(2,1)S(1)} %bitcast.10, s32[1,128]{1,0:T(1,128)S(1)} %copy-done.5, s32[1,128]{1,0:T(1,128)S(1)} %bitcast.15, f32[1,4096]{1,0:T(1,128)S(1)} %bitcast.14, bf16[2,4,4096]{2,1,0:T(4,128)(2,1)S(1)} %bitcast.13, bf16[448,1024]{1,0:T(8,128)(2,1)S(1)} %bitcast.11, ...), custom_call_target="tpu_custom_call" | custom-call | tf_op jit(solution)/shard_map/pallas_call | solution.py:344
  125.2 0.7 copy.9
Async XLA Ops:
  0.0 0.7 copy-start.5
  0.0 0.7 copy-start.6
  0.7 1.2 copy-start
  1.9 1.2 copy-start.1
  3.1 1.2 copy-start.2
  4.3 0.8 copy-start.3
  5.1 0.7 copy-start.4

commit v2 on v1

--- a/solution.py
+++ b/solution.py
@@ -15,17 +15,18 @@
 
 def kernel(
     n_pipe, n_dp,
-    tokens, modality, routes, gain, router, gate_hbm, down_hbm,
+    tokens, modality_hbm, routes_hbm, gain_hbm, router_hbm, gate_hbm, down_hbm,
     out,
-    tok_v, normed_v, gate_v, down_v, arrived, stat_tx, stat_rx, placer, unplacer, chosen,
-    packed, recv, rs_tx, rs_rx, own_sum, hid, term, ret_far, ret_near, fin,
+    modality, routes, gain, router, tok_v, normed_v, gate_v, down_v, arrived, stat_tx, stat_rx, placer, unplacer, chosen,
+    packed, recv, sum_tx, sum_half, sum_rx, own_sum, hid, term, ret_far, ret_near, fin,
     local_sem, pipe_send, pipe_recv, first_send, forward_send, dispatch_recv,
-    sum_send, sum_recv, hid_send, hid_recv, ret_send, far_recv, near_recv, fin_recv,
+    half_send, half_recv, sum_send, sum_recv, hid_send, hid_recv, relay_send, relay_recv, ret_send, far_recv, near_recv, fin_recv,
 ):
     tok = tok_v.shape[0]
     cap = recv.shape[1] // 2
     part = recv.shape[2]
-    piece = rs_rx.shape[2]
+    piece = sum_rx.shape[2]
+    half = piece // 2
     s, j, d = lax.axis_index("pipe"), lax.axis_index("expert"), lax.axis_index("dp")
     xl, z = j // Z, j % Z
     g, p = z // 4, z % 4
@@ -54,6 +55,12 @@
     tok_copy = pltpu.make_async_copy(tokens, tok_v, local_sem.at[0])
     gate_copy = pltpu.make_async_copy(gate_hbm, gate_v, local_sem.at[1])
     down_copy = pltpu.make_async_copy(down_hbm, down_v, local_sem.at[2])
+    small = [
+        pltpu.make_async_copy(a, b, local_sem.at[3 + k])
+        for k, (a, b) in enumerate(((modality_hbm, modality), (routes_hbm, routes), (gain_hbm, gain), (router_hbm, router)))
+    ]
+    for copy in small:
+        copy.start()
     tok_copy.start()
 
     barrier = pltpu.get_barrier_semaphore()
@@ -61,11 +68,13 @@
         ((s + 1) % n_pipe, j, d),
         ((s + n_pipe - 1) % n_pipe, j, d),
         at(other, z), at(xl, near), at(xl, far), at(xl, second), at(other, second), at(other, beside),
-    ] + [(s, j, (d + k) % n_dp) for k in range(1, n_dp)]
+    ] + [(s, j, (d + k) % n_dp) for k in (1, n_dp - 1)]
     for device in partners:
         pl.semaphore_signal(barrier, inc=1, device_id=device, device_id_type=MESH)
     gate_copy.start()
     down_copy.start()
+    for copy in small:
+        copy.wait()
 
     route_row = routes[...]
     hits = (lax.broadcasted_iota(jnp.int32, (8, tok), 0) == route_row).astype(jnp.float32)
@@ -123,21 +132,20 @@
     packed[0] = pack(other, g)
     cross = send(packed.at[0], rows(recv, z, xl), first_send.at[0], dispatch_recv.at[z, xl], at(other, z))
     cross.start()
-    recv[z, pl.ds(pl.multiple_of(xl * cap, cap), cap), :] = pack(xl, g)
-    own_far = send(rows(recv, z, xl), rows(recv, z, xl), first_send.at[1], dispatch_recv.at[z, xl], at(xl, far))
-    own_near = send(rows(recv, z, xl), rows(recv, z, xl), first_send.at[2], dispatch_recv.at[z, xl], at(xl, near))
-    own_far.start()
-
-    @pl.when(is_mid)
-    def _():
-        own_near.start()
-
     packed[1] = pack(xl, 1 - g)
     ext_own = send(packed.at[1], rows(recv, z, xl), first_send.at[3], dispatch_recv.at[z, xl], at(xl, across))
     ext_own.start()
     packed[2] = pack(other, 1 - g)
     ext_other = send(packed.at[2], rows(recv, z, xl), first_send.at[4], dispatch_recv.at[z, xl], at(other, across))
     ext_other.start()
+    recv[z, pl.ds(pl.multiple_of(xl * cap, cap), cap), :] = pack(xl, g)
+    own_far = send(rows(recv, z, xl), rows(recv, z, xl), first_send.at[1], dispatch_recv.at[z, xl], at(xl, far))
+    own_near = send(rows(recv, z, xl), rows(recv, z, xl), first_send.at[2], dispatch_recv.at[z, xl], at(xl, near))
+    own_far.start()
+
+    @pl.when(is_mid)
+    def _():
+        own_near.start()
 
     relay_far = send(rows(recv, z, other), rows(recv, z, other), first_send.at[5], dispatch_recv.at[z, other], at(xl, far))
     relay_near = send(rows(recv, z, other), rows(recv, z, other), first_send.at[6], dispatch_recv.at[z, other], at(xl, near))
@@ -152,29 +160,50 @@
     down_copy.wait()
 
     def source(t):
-        late = (1 - mid) * (t // 5)
-        usual = (t % 2) * ((t + 1) // 2) - (1 - t % 2) * (t // 2)
-        offset = usual * (1 - late) + late * (2 - t)
+        from1, from3, from5, from6 = (t + 7) // 8, (t + 5) // 8, (t + 3) // 8, (t + 2) // 8
+        offset = (
+            (from1 - from3) * (t + mid)
+            + (from3 - from5) * (mid - t - 1)
+            + (from5 - from6) * (4 * mid - 3)
+            + from6 * (t - 8)
+        )
         return (z + nd * offset + 2 * Z) % Z
 
     def forward(t, zz, x):
-        to_near = mid * (1 - (t % 2) * (1 - t // 7))
+        to_near = mid * ((t + 5) // 8 - (t + 3) // 8 + (t + 2) // 8)
         target = (z + nd * (2 * to_near - 1) + Z) % Z
         return send(rows(recv, zz, x), rows(recv, zz, x), forward_send.at[t, x], dispatch_recv.at[zz, x], at(xl, target))
 
     def forwards(t):
-        return (t >= 1) & (is_mid | (t == 1) | (t == 3))
-
-    def sum_copy(t, k):
-        q = (d + k) % n_dp
+        return (t >= 1) & (is_mid | (t <= 2))
+
+    ways = (0, 1)
+
+    def beyond(way):
+        return (d + 1 - 2 * way + n_dp) % n_dp
+
+    def span(ref, t, q, start, count):
+        return ref.at[t, pl.ds(pl.multiple_of(q * piece + start, half), count)]
+
+    def half_copy(t, way):
         return send(
-            rs_tx.at[t, pl.ds(pl.multiple_of(q * piece, piece), piece)], rs_rx.at[t, k - 1],
-            sum_send.at[t, k - 1], sum_recv.at[t, k - 1], (s, j, q),
+            span(sum_tx, t, (d + 2) % n_dp, way * half, half), sum_half.at[t, way],
+            half_send.at[t, way], half_recv.at[t, way], (s, j, beyond(way)),
         )
 
-    def hid_copy(t, k):
-        own = hid.at[t, pl.ds(pl.multiple_of(d * piece, piece), piece)]
-        return send(own, own, hid_send.at[t, k - 1], hid_recv.at[t, k - 1], (s, j, (d + k) % n_dp))
+    def sum_copy(t, way):
+        return send(
+            span(sum_tx, t, beyond(way), 0, piece), sum_rx.at[t, way],
+            sum_send.at[t, way], sum_recv.at[t, way], (s, j, beyond(way)),
+        )
+
+    def hid_copy(t, way):
+        own = span(hid, t, d, 0, piece)
+        return send(own, own, hid_send.at[t, way], hid_recv.at[t, way], (s, j, beyond(way)))
+
+    def relay_copy(t, way):
+        passed = span(hid, t, beyond(1 - way), way * half, half)
+        return send(passed, passed, relay_send.at[t, way], relay_recv.at[t, way], (s, j, beyond(way)))
 
     def leaf_copy(zz, x):
         return send(rows(ret_near, zz, x), rows(ret_near, zz, x), ret_send.at[zz, x], near_recv.at[zz, x], at(xl, far))
@@ -207,85 +236,100 @@
                 recv[zz], gate_v[...], (((1,), (1,)), ((), ())), preferred_element_type=jnp.float32
             )
             own_sum[i % 2] = terms
-            rs_tx[i] = terms.astype(jnp.bfloat16)
-            for k in range(1, n_dp):
-                sum_copy(i, k).start()
+            sum_tx[i] = terms.astype(jnp.bfloat16)
+            for way in ways:
+                half_copy(i, way).start()
 
         @pl.when((i >= 1) & (i <= 8))
         def _():
             t = i - 1
-            for k in range(1, n_dp):
-                sum_copy(t, k).wait_recv()
             mine = pl.ds(pl.multiple_of(d * piece, piece), piece)
             total = own_sum[t % 2, mine, :]
-            for k in range(1, n_dp):
-                total = total + rs_rx[t, k - 1].astype(jnp.float32)
+            for way in ways:
+                sum_copy(t, way).wait_recv()
+                total = total + sum_rx[t, way].astype(jnp.float32)
             hid[t, mine, :] = (total / (1.0 + jnp.exp(-total))).astype(jnp.bfloat16)
-            for k in range(1, n_dp):
-                hid_copy(t, k).start()
+            for way in ways:
+                hid_copy(t, way).start()
 
         @pl.when((i >= 2) & (i <= 9))
         def _():
             t = i - 2
             zz = source(t)
-            for k in range(1, n_dp):
-                hid_copy(t, k).wait_recv()
+            for way in ways:
+                relay_copy(t, way).wait_recv()
             term[zz] = jnp.dot(hid[t], down_v[...], preferred_element_type=jnp.float32)
 
-            @pl.when(is_end & ((t == 2) | (t >= 4)))
+            @pl.when(is_end & (t >= 3))
             def _():
                 ret_near[zz] = term[zz].astype(jnp.bfloat16)
                 for x in range(2):
                     leaf_copy(zz, x).start()
 
+        @pl.when(i <= 7)
+        def _():
+            for way in ways:
+                half_copy(i, way).wait_recv()
+                joined = pl.ds(pl.multiple_of(beyond(way) * piece + way * half, half), half)
+                sum_tx[i, joined, :] = (own_sum[i % 2, joined, :] + sum_half[i, way].astype(jnp.float32)).astype(jnp.bfloat16)
+                sum_copy(i, way).start()
+
+        @pl.when((i >= 1) & (i <= 8))
+        def _():
+            for way in ways:
+                hid_copy(i - 1, way).wait_recv()
+                relay_copy(i - 1, way).start()
+
         @pl.when(is_mid & (i >= 7) & (i <= 10))
         def _():
-            zz = (z - nd * (i - 6) + Z) % Z
+            u = i - 7
+            zz = (z + nd * ((u // 2) * (2 * u - 1) - 3 - u) + Z) % Z
             for x in range(2):
                 leaf_copy(zz, x).wait_recv()
-                span = slice(x * cap, (x + 1) * cap)
-                ret_near[zz, span] = (term[zz, span] + ret_near[zz, span].astype(jnp.float32)).astype(jnp.bfloat16)
+                block = slice(x * cap, (x + 1) * cap)
+                ret_near[zz, block] = (term[zz, block] + ret_near[zz, block].astype(jnp.float32)).astype(jnp.bfloat16)
                 up_copy(zz, x).start()
 
-        @pl.when(is_mid & (i >= 9) & (i <= 11))
-        def _():
-            zz = (z + nd * (i - 8) + Z) % Z
+        @pl.when(is_mid & (i >= 8) & (i <= 10))
+        def _():
+            v = i - 8
+            zz = (z + nd * (2 + v - 3 * (v // 2)) + Z) % Z
             for x in range(2):
                 down_chain(zz, x).wait_recv()
-                span = slice(x * cap, (x + 1) * cap)
-                ret_far[zz, span] = (term[zz, span] + ret_far[zz, span].astype(jnp.float32)).astype(jnp.bfloat16)
+                block = slice(x * cap, (x + 1) * cap)
+                ret_far[zz, block] = (term[zz, block] + ret_far[zz, block].astype(jnp.float32)).astype(jnp.bfloat16)
                 down_chain(zz, x).start()
 
-        @pl.when((is_mid & (i == 8)) | (is_end & (i == 10)))
+        @pl.when(i == 11)
         def _():
             for x in (other, xl):
-                span = pl.ds(pl.multiple_of(x * cap, cap), cap)
+                block = pl.ds(pl.multiple_of(x * cap, cap), cap)
                 up_copy(z, x).wait_recv()
-                ret_far[z, span, :] = (term[z, span, :] + ret_far[z, span, :].astype(jnp.float32)).astype(jnp.bfloat16)
+                ret_far[z, block, :] = (term[z, block, :] + ret_far[z, block, :].astype(jnp.float32)).astype(jnp.bfloat16)
 
                 @pl.when(is_mid)
                 def _():
                     leaf_copy(z, x).wait_recv()
-                    ret_far[z, span, :] = (
-                        ret_far[z, span, :].astype(jnp.float32) + ret_near[z, span, :].astype(jnp.float32)
+                    ret_far[z, block, :] = (
+                        ret_far[z, block, :].astype(jnp.float32) + ret_near[z, block, :].astype(jnp.float32)
                     ).astype(jnp.bfloat16)
 
                 if x is other:
                     home_copy(z, other).start()
             fin[own_expert] = ret_far[z, pl.ds(pl.multiple_of(xl * cap, cap), cap), :]
 
-        @pl.when(is_end & (i >= 11))
-        def _():
-            zz = (z + nd * (i - 10) + Z) % Z
+        @pl.when(is_end & ((i == 9) | (i == 10)))
+        def _():
+            zz = (z + nd * (i - 8) + Z) % Z
             for x in range(2):
                 up_copy(zz, x).wait_recv()
-                span = slice(x * cap, (x + 1) * cap)
-                ret_far[zz, span] = (term[zz, span] + ret_far[zz, span].astype(jnp.float32)).astype(jnp.bfloat16)
+                block = slice(x * cap, (x + 1) * cap)
+                ret_far[zz, block] = (term[zz, block] + ret_far[zz, block].astype(jnp.float32)).astype(jnp.bfloat16)
                 home_copy(zz, x).start()
 
         return carry
 
-    lax.fori_loop(0, 13, each_step, 0)
+    lax.fori_loop(0, 12, each_step, 0)
 
     for x, group in ((other, g), (xl, 1 - g), (other, 1 - g)):
         e = 2 * x + group
@@ -315,9 +359,11 @@
             for x in range(2):
                 forward(t, zz, x).wait_send()
 
-        for k in range(1, n_dp):
-            sum_copy(t, k).wait_send()
-            hid_copy(t, k).wait_send()
+        for way in ways:
+            half_copy(t, way).wait_send()
+            sum_copy(t, way).wait_send()
+            hid_copy(t, way).wait_send()
+            relay_copy(t, way).wait_send()
 
         @pl.when(t >= 1)
         def _():
@@ -344,9 +390,13 @@
     result = pl.pallas_call(
         functools.partial(kernel, n_pipe, n_dp),
         out_shape=jax.ShapeDtypeStruct((tok, part), bf16),
-        in_specs=[anywhere, vmem, vmem, vmem, vmem, anywhere, anywhere],
+        in_specs=[anywhere] * 7,
         out_specs=vmem,
         scratch_shapes=[
+            pltpu.VMEM((1, tok), jnp.int32),
+            pltpu.VMEM((1, tok), jnp.int32),
+            pltpu.VMEM((1, width), f32),
+            pltpu.VMEM((router.shape[0], router.shape[2], width), bf16),
             pltpu.VMEM((tok, width), bf16),
             pltpu.VMEM((tok, width), bf16),
             pltpu.VMEM((hidden, part), bf16),
@@ -360,30 +410,35 @@
             pltpu.VMEM((3, cap, part), bf16),
             pltpu.VMEM((STEPS, 2 * cap, part), bf16),
             pltpu.VMEM((STEPS, 2 * cap, hidden), bf16),
-            pltpu.VMEM((STEPS, n_dp - 1, piece, hidden), bf16),
+            pltpu.VMEM((STEPS, 2, piece // 2, hidden), bf16),
+            pltpu.VMEM((STEPS, 2, piece, hidden), bf16),
             pltpu.VMEM((2, 2 * cap, hidden), f32),
             pltpu.VMEM((STEPS, 2 * cap, hidden), bf16),
             pltpu.VMEM((STEPS, 2 * cap, part), f32),
             pltpu.VMEM((STEPS, 2 * cap, part), bf16),
             pltpu.VMEM((STEPS, 2 * cap, part), bf16),
             pltpu.VMEM((4, cap, part), bf16),
-            dma((3,)),
+            dma((7,)),
             dma((2,)),
             dma((2,)),
             dma((7,)),
             dma((STEPS, 2)),
             dma((STEPS, 2)),
-            dma((STEPS, n_dp - 1)),
-            dma((STEPS, n_dp - 1)),
-            dma((STEPS, n_dp - 1)),
-            dma((STEPS, n_dp - 1)),
+            dma((STEPS, 2)),
+            dma((STEPS, 2)),
+            dma((STEPS, 2)),
+            dma((STEPS, 2)),
+            dma((STEPS, 2)),
+            dma((STEPS, 2)),
+            dma((STEPS, 2)),
+            dma((STEPS, 2)),
             dma((STEPS, 2)),
             dma((STEPS, 2)),
             dma((STEPS, 2)),
             dma((4,)),
         ],
         compiler_params=pltpu.CompilerParams(
-            collective_id=0, has_side_effects=True, vmem_limit_bytes=48 * 1024 * 1024
+            collective_id=0, has_side_effects=True, vmem_limit_bytes=60 * 1024 * 1024
         ),
     )(
         tokens[0],

time: 126 us -> 129 us (1.024)
  the two profiles are of different devices: /device:TPU:64 before, /device:TPU:110 now
where the time goes in v2:
time: 129 us
  Pallas kernels  128 us (99%)
  local copies, waits for them, and re-layouts  1.67 us (1%)
    pallas_call x1, Pallas kernels, local(): pl.pallas_call(functools.partial(kernel, n_pipe, n_dp), out_shape=jax.Sha...  128 us

profile of v2, /device:TPU:110, one launch (start us, length us, event | category | flops | bytes accessed | tf_op | source)
XLA Modules:
  0.0 129.2 jit_solution(5698794093517526902)
XLA Ops:
  0.0 127.5 %shard_map.73 = bf16[128,1024]{1,0:T(8,128)(2,1)} custom-call(bf16[128,4096]{1,0:T(8,128)(2,1)} %bitcast.10, s32[1,128]{1,0:T(1,128)} %modality_hbm.1, s32[1,128]{1,0:T(1,128)} %bitcast.15, f32[1,4096]{1,0:T(1,128)} %bitcast.14, bf16[2,4,4096]{2,1,0:T(4,128)(2,1)} %bitcast.13, bf16[448,1024]{1,0:T(8,128)(2,1)} %bitcast.11, bf16[448,1024]{1,0:T(8,128)(2,1)} %bitcast.12), custom_call_target="tpu_custom_call" | custom-call | tf_op jit(solution)/shard_map/pallas_call | solution.py:390
  127.5 1.7 %copy.9 = bf16[1,128,1024]{2,1,0:T(8,128)(2,1)} copy(bf16[1,128,1024]{2,1,0:T(8,128)(2,1)} %bitcast.9) | data formatting | bytes 524288

commit v3 on v2

v3 whole, which is shorter than its diff:
```python
import functools

import jax
import jax.numpy as jnp
from jax import lax
from jax.experimental import pallas as pl
from jax.experimental.pallas import tpu as pltpu
from jax.sharding import PartitionSpec as P

MESH = pl.DeviceIdType.MESH
epsilon = 1e-06
Z = 8
STEPS = 8


def kernel(
    n_pipe, n_dp,
    tokens, modality_hbm, routes_hbm, gain_hbm, router_hbm, gate_hbm, down_hbm,
    out,
    modality, routes, gain, router, tok_v, normed_v, gate_v, down_v, arrived, stat_tx, stat_rx, placer, unplacer, chosen,
    packed, recv, sum_tx, sum_half, sum_rx, own_sum, hid, term, ret_tx, joint, own_rx, fin, summed,
    local_sem, pipe_send, pipe_recv, first_send, forward_send, dispatch_recv,
    half_send, half_recv, sum_send, sum_recv, hid_send, hid_recv, relay_send, relay_recv, ret_send, joint_recv, own_recv, fin_recv,
):
    tok = tok_v.shape[0]
    cap = recv.shape[1] // 2
    part = recv.shape[2]
    piece = sum_rx.shape[2]
    half = piece // 2
    s, j, d = lax.axis_index("pipe"), lax.axis_index("expert"), lax.axis_index("dp")
    xl, z = j // Z, j % Z
    g, p = z // 4, z % 4
    mid = ((p + 1) // 2) % 2
    nd = 2 * (p // 2) - 1
    near, far, far2 = (z + nd + Z) % Z, (z - nd + Z) % Z, (z - 2 * nd + Z) % Z
    entry = (z + nd * (1 + mid) + Z) % Z
    inner = (z + nd * (3 + mid) + Z) % Z
    other = 1 - xl
    is_mid = mid == 1
    is_end = mid == 0

    def at(x, zz):
        return (s, x * Z + zz, d)

    def send(src, dst, send_sem, recv_sem, device):
        return pltpu.make_async_remote_copy(
            src_ref=src, dst_ref=dst, send_sem=send_sem, recv_sem=recv_sem,
            device_id=device, device_id_type=MESH,
        )

    def rows(ref, zz, x):
        return ref.at[zz, pl.ds(pl.multiple_of(x * cap, cap), cap)]

    tok_copy = pltpu.make_async_copy(tokens, tok_v, local_sem.at[0])
    gate_copy = pltpu.make_async_copy(gate_hbm, gate_v, local_sem.at[1])
    down_copy = pltpu.make_async_copy(down_hbm, down_v, local_sem.at[2])
    small = [
        pltpu.make_async_copy(a, b, local_sem.at[3 + k])
        for k, (a, b) in enumerate(((modality_hbm, modality), (routes_hbm, routes), (gain_hbm, gain), (router_hbm, router)))
    ]
    for copy in small:
        copy.start()
    tok_copy.start()

    barrier = pltpu.get_barrier_semaphore()
    partners = [
        ((s + 1) % n_pipe, j, d),
        ((s + n_pipe - 1) % n_pipe, j, d),
        (s, j, (d + 1) % n_dp),
        (s, j, (d + n_dp - 1) % n_dp),
        at(other, z), at(xl, far), at(xl, far2),
    ]
    for steps in (1 + mid, 2 + 2 * mid, 3 - 6 * mid):
        partners += [at(x, (z + nd * steps + Z) % Z) for x in (xl, other)]
    for device in partners:
        pl.semaphore_signal(barrier, inc=1, device_id=device, device_id_type=MESH)

    @pl.when(is_mid)
    def _():
        pl.semaphore_signal(barrier, inc=1, device_id=at(xl, near), device_id_type=MESH)

    gate_copy.start()
    down_copy.start()
    for copy in small:
        copy.wait()

    route_row = routes[...]
    hits = (lax.broadcasted_iota(jnp.int32, (8, tok), 0) == route_row).astype(jnp.float32)
    before = (
        lax.broadcasted_iota(jnp.int32, (tok, tok), 0) < lax.broadcasted_iota(jnp.int32, (tok, tok), 1)
    ).astype(jnp.bfloat16)
    earlier = jnp.dot(hits.astype(jnp.bfloat16), before, preferred_element_type=jnp.float32)
    rank = jnp.sum(hits * earlier, axis=0, keepdims=True)
    slot_row = route_row.astype(jnp.float32) * cap + rank
    slots = lax.broadcasted_iota(jnp.int32, (4 * cap, tok), 0).astype(jnp.float32)
    placer[...] = (slots == slot_row).astype(jnp.bfloat16)
    slot_col = jnp.transpose(jnp.broadcast_to(slot_row, (tok, tok)))[:, 0:1]
    slots = lax.broadcasted_iota(jnp.int32, (tok, 4 * cap), 1).astype(jnp.float32)
    unplacer[...] = (slots == slot_col).astype(jnp.bfloat16)
    pick_row = (modality[...] * 4 + route_row).astype(jnp.float32)
    pick_col = jnp.transpose(jnp.broadcast_to(pick_row, (tok, tok)))[:, 0:1]
    lanes = lax.broadcasted_iota(jnp.int32, (tok, 128), 1).astype(jnp.float32)
    chosen[...] = (lanes == pick_col).astype(jnp.float32)

    pl.semaphore_wait(barrier, len(partners) + mid)

    following = ((s + 1) % n_pipe, j, d)
    own_columns = pl.ds(pl.multiple_of(d * part, part), part)
    raw_copy = send(tokens.at[:, own_columns], arrived, pipe_send.at[0], pipe_recv.at[0], following)
    raw_copy.start()

    stat_tx[...] = jnp.zeros_like(stat_tx)
    tok_copy.wait()

    def norm_rows(i, carry):
        block = pl.ds(pl.multiple_of(i * 16, 16), 16)
        x = tok_v[block, :].astype(jnp.float32)
        scale = lax.rsqrt(jnp.mean(x * x, axis=-1, keepdims=True) + epsilon)
        normed_v[block, :] = (x * scale * gain[...]).astype(jnp.bfloat16)
        stat_tx[block, 8:9] = scale
        return carry

    lax.fori_loop(0, tok // 16, norm_rows, 0)
    for kind in range(2):
        stat_tx[:, 4 * kind : 4 * kind + 4] = lax.dot_general(
            normed_v[...], router[kind], (((1,), (1,)), ((), ())), preferred_element_type=jnp.float32
        )
    stat_copy = send(stat_tx, stat_rx, pipe_send.at[1], pipe_recv.at[1], following)
    stat_copy.start()
    raw_copy.wait_recv()
    stat_copy.wait_recv()

    scale = stat_rx[:, 8:9]
    normed = (arrived[...].astype(jnp.float32) * scale * gain[:, own_columns]).astype(jnp.bfloat16)

    def pack(x, group):
        spot = pl.ds(pl.multiple_of((2 * x + group) * cap, cap), cap)
        return jnp.dot(placer[spot, :], normed, preferred_element_type=jnp.float32).astype(jnp.bfloat16)

    packed[0] = pack(other, g)
    cross = send(packed.at[0], rows(recv, z, xl), first_send.at[0], dispatch_recv.at[z, xl], at(other, z))
    cross.start()
    def spread(src, x, targets, first):
        return [
            send(src, rows(recv, z, xl), first_send.at[first + k], dispatch_recv.at[z, xl], at(x, target))
            for k, target in enumerate(targets)
        ]

    packed[1] = pack(xl, 1 - g)
    ext_own = spread(packed.at[1], xl, (entry, inner), 1)
    for copy in ext_own:
        copy.start()
    packed[2] = pack(other, 1 - g)
    ext_other = spread(packed.at[2], other, (entry, inner), 3)
    for copy in ext_other:
        copy.start()
    recv[z, pl.ds(pl.multiple_of(xl * cap, cap), cap), :] = pack(xl, g)

    def inside(x, first):
        block = rows(recv, z, x)
        return [
            send(block, block, first_send.at[first + k], dispatch_recv.at[z, x], at(xl, target))
            for k, target in enumerate((far, far2, near))
        ]

    own_sends, relay_sends = inside(xl, 5), inside(other, 8)

    def start_inside(copies):
        copies[0].start()
        copies[1].start()

        @pl.when(is_mid)
        def _():
            copies[2].start()

    start_inside(own_sends)
    relay_sends[0].wait_recv()
    start_inside(relay_sends)

    gate_copy.wait()
    down_copy.wait()

    def source(t):
        from1, from3, from4, from6, from7 = (t + 7) // 8, (t + 5) // 8, (t + 4) // 8, (t + 2) // 8, (t + 1) // 8
        at_end = (from1 - from3) * t - (from3 - from6) * t - (from6 - from7) * 2 - from7
        at_mid = -(from1 - from4) * (t + 1) + (from4 - from6) * (t - 2) + (from6 - from7) - from7
        return (z + nd * (mid * at_mid + (1 - mid) * at_end) + 2 * Z) % Z

    def forward(t, zz, x):
        target = mid * near + (1 - mid) * far
        return send(rows(recv, zz, x), rows(recv, zz, x), forward_send.at[t, x], dispatch_recv.at[zz, x], at(xl, target))

    def forwards(t):
        return (t >= 1) & (t <= 2 + mid)

    ways = (0, 1)

    def beyond(way):
        return (d + 1 - 2 * way + n_dp) % n_dp

    def span(ref, t, q, start, count):
        return ref.at[t, pl.ds(pl.multiple_of(q * piece + start, half), count)]

    def half_copy(t, way):
        return send(
            span(sum_tx, t, (d + 2) % n_dp, way * half, half), sum_half.at[t, way],
            half_send.at[t, way], half_recv.at[t, way], (s, j, beyond(way)),
        )

    def sum_copy(t, way):
        return send(
            span(sum_tx, t, beyond(way), 0, piece), sum_rx.at[t, way],
            sum_send.at[t, way], sum_recv.at[t, way], (s, j, beyond(way)),
        )

    def hid_copy(t, way):
        own = span(hid, t, d, 0, piece)
        return send(own, own, hid_send.at[t, way], hid_recv.at[t, way], (s, j, beyond(way)))

    def relay_copy(t, way):
        passed = span(hid, t, beyond(1 - way), way * half, half)
        return send(passed, passed, relay_send.at[t, way], relay_recv.at[t, way], (s, j, beyond(way)))

    own_expert = 2 * xl + g

    def joint_copy(zz, x):
        target = mid * near + (1 - mid) * far
        return send(rows(ret_tx, zz, x), rows(joint, zz, x), ret_send.at[zz, x], joint_recv.at[zz, x], at(xl, target))

    def root_copy(zz, x, place, target):
        return send(rows(ret_tx, zz, x), rows(own_rx, place, x), ret_send.at[zz, x], own_recv.at[place, x], at(xl, target))

    def home_copy(zz, x, place):
        return send(rows(ret_tx, zz, x), fin.at[own_expert, place], ret_send.at[zz, x], fin_recv.at[own_expert, place], at(x, zz))

    def each_step(i, carry):
        @pl.when(i <= 7)
        def _():
            zz = source(i)
            for x in (xl, other):
                @pl.when(i >= 1)
                def _():
                    forward(i, zz, x).wait_recv()

                @pl.when(forwards(i))
                def _():
                    forward(i, zz, x).start()

            terms = lax.dot_general(
                recv[zz], gate_v[...], (((1,), (1,)), ((), ())), preferred_element_type=jnp.float32
            )
            own_sum[i % 4] = terms
            sum_tx[i] = terms.astype(jnp.bfloat16)
            for way in ways:
                half_copy(i, way).start()

        @pl.when((i >= 1) & (i <= 8))
        def _():
            t = i - 1
            for way in ways:
                half_copy(t, way).wait_recv()
                joined = pl.ds(pl.multiple_of(beyond(way) * piece + way * half, half), half)
                sum_tx[t, joined, :] = (own_sum[t % 4, joined, :] + sum_half[t, way].astype(jnp.float32)).astype(jnp.bfloat16)
                sum_copy(t, way).start()

        @pl.when((i >= 2) & (i <= 9))
        def _():
            t = i - 2
            mine = pl.ds(pl.multiple_of(d * piece, piece), piece)
            total = own_sum[t % 4, mine, :]
            for way in ways:
                sum_copy(t, way).wait_recv()
                total = total + sum_rx[t, way].astype(jnp.float32)
            hid[t, mine, :] = (total / (1.0 + jnp.exp(-total))).astype(jnp.bfloat16)
            for way in ways:
                hid_copy(t, way).start()

        @pl.when((i >= 3) & (i <= 10))
        def _():
            for way in ways:
                hid_copy(i - 3, way).wait_recv()
                relay_copy(i - 3, way).start()

        @pl.when(i >= 4)
        def _():
            t = i - 4
            zz = source(t)
            for way in ways:
                relay_copy(t, way).wait_recv()
            term[zz] = jnp.dot(hid[t], down_v[...], preferred_element_type=jnp.float32)

            @pl.when(t >= 3 + mid)
            def _():
                ret_tx[zz] = term[zz].astype(jnp.bfloat16)

            for x in range(2):
                @pl.when((t >= 3 + mid) & (t <= 5))
                def _():
                    joint_copy(zz, x).start()

                @pl.when(t == 6)
                def _():
                    root_copy(zz, x, 2 - mid, mid * near + (1 - mid) * far2).start()

                @pl.when(t == 7)
                def _():
                    root_copy(zz, x, mid, far).start()

        @pl.when((i >= 9 - mid) & (i <= 10))
        def _():
            zz = (z + nd * (mid * (6 - i) + (1 - mid) * (i - 8)) + 2 * Z) % Z
            for x in range(2):
                block = slice(x * cap, (x + 1) * cap)
                joint_copy(zz, x).wait_recv()
                ret_tx[zz, block] = (term[zz, block] + joint[zz, block].astype(jnp.float32)).astype(jnp.bfloat16)

                @pl.when(i == 8)
                def _():
                    root_copy(zz, x, 2, far2).start()

                @pl.when(i >= 9)
                def _():
                    home_copy(zz, x, mid).start()

        return carry

    lax.fori_loop(0, 12, each_step, 0)

    for x in (other, xl):
        block = pl.ds(pl.multiple_of(x * cap, cap), cap)
        for place in (1, 2):
            root_copy(z, x, place, far).wait_recv()
        ret_tx[z, block, :] = (
            term[z, block, :] + own_rx[1, block, :].astype(jnp.float32) + own_rx[2, block, :].astype(jnp.float32)
        ).astype(jnp.bfloat16)

        @pl.when(is_mid)
        def _():
            root_copy(z, x, 0, near).wait_recv()
            ret_tx[z, block, :] = (
                term[z, block, :] + own_rx[0, block, :].astype(jnp.float32)
                + own_rx[1, block, :].astype(jnp.float32) + own_rx[2, block, :].astype(jnp.float32)
            ).astype(jnp.bfloat16)

        if x is other:
            home_copy(z, other, 0).start()
    summed[pl.ds(pl.multiple_of(own_expert * cap, cap), cap), :] = ret_tx[z, pl.ds(pl.multiple_of(xl * cap, cap), cap), :]

    def arrival(e, place):
        return send(fin.at[e, place], fin.at[e, place], ret_send.at[0, 0], fin_recv.at[e, place], at(other, z))

    for x in (xl, other):
        e = 2 * x + 1 - g
        for place in range(2):
            arrival(e, place).wait_recv()
        summed[pl.ds(pl.multiple_of(e * cap, cap), cap), :] = (
            fin[e, 0].astype(jnp.float32) + fin[e, 1].astype(jnp.float32)
        ).astype(jnp.bfloat16)
    e = 2 * other + g
    arrival(e, 0).wait_recv()
    summed[pl.ds(pl.multiple_of(e * cap, cap), cap), :] = fin[e, 0]

    gate_value = 1.0 / (1.0 + jnp.exp(-jnp.sum(chosen[...] * stat_rx[...], axis=1, keepdims=True)))
    expert_out = jnp.dot(
        unplacer[...], summed[...], preferred_element_type=jnp.float32
    )
    out[...] = (arrived[...].astype(jnp.float32) + gate_value * expert_out).astype(jnp.bfloat16)

    raw_copy.wait_send()
    stat_copy.wait_send()
    for copy in [cross] + ext_own + ext_other + own_sends[:2] + relay_sends[:2]:
        copy.wait_send()

    @pl.when(is_mid)
    def _():
        own_sends[2].wait_send()
        relay_sends[2].wait_send()

    def sent(t, carry):
        zz = source(t)

        @pl.when(forwards(t))
        def _():
            for x in range(2):
                forward(t, zz, x).wait_send()

        for way in ways:
            half_copy(t, way).wait_send()
            sum_copy(t, way).wait_send()
            hid_copy(t, way).wait_send()
            relay_copy(t, way).wait_send()

        @pl.when(t >= 1)
        def _():
            for x in range(2):
                joint_copy(zz, x).wait_send()

        return carry

    lax.fori_loop(0, STEPS, sent, 0)
    home_copy(z, other, 0).wait_send()


def local(tokens, modality, routes, norm_gain, router, gate_weight, down_weight):
    tok, width = tokens.shape[1:]
    n_pipe, n_dp = lax.axis_size("pipe"), lax.axis_size("dp")
    part = width // n_dp
    cap = 2 * tok // router.shape[2]
    hidden = gate_weight.shape[2]
    piece = 2 * cap // n_dp
    bf16, f32 = jnp.bfloat16, jnp.float32
    vmem = pl.BlockSpec(memory_space=pltpu.VMEM)
    anywhere = pl.BlockSpec(memory_space=pl.ANY)
    dma = pltpu.SemaphoreType.DMA
    result = pl.pallas_call(
        functools.partial(kernel, n_pipe, n_dp),
        out_shape=jax.ShapeDtypeStruct((tok, part), bf16),
        in_specs=[anywhere] * 7,
        out_specs=vmem,
        scratch_shapes=[
            pltpu.VMEM((1, tok), jnp.int32),
            pltpu.VMEM((1, tok), jnp.int32),
            pltpu.VMEM((1, width), f32),
            pltpu.VMEM((router.shape[0], router.shape[2], width), bf16),
            pltpu.VMEM((tok, width), bf16),
            pltpu.VMEM((tok, width), bf16),
            pltpu.VMEM((hidden, part), bf16),
            pltpu.VMEM((hidden, part), bf16),
            pltpu.VMEM((tok, part), bf16),
            pltpu.VMEM((tok, 128), f32),
            pltpu.VMEM((tok, 128), f32),
            pltpu.VMEM((4 * cap, tok), bf16),
            pltpu.VMEM((tok, 4 * cap), bf16),
            pltpu.VMEM((tok, 128), f32),
            pltpu.VMEM((3, cap, part), bf16),
            pltpu.VMEM((STEPS, 2 * cap, part), bf16),
            pltpu.VMEM((STEPS, 2 * cap, hidden), bf16),
            pltpu.VMEM((STEPS, 2, piece // 2, hidden), bf16),
            pltpu.VMEM((STEPS, 2, piece, hidden), bf16),
            pltpu.VMEM((4, 2 * cap, hidden), f32),
            pltpu.VMEM((STEPS, 2 * cap, hidden), bf16),
            pltpu.VMEM((STEPS, 2 * cap, part), f32),
            pltpu.VMEM((STEPS, 2 * cap, part), bf16),
            pltpu.VMEM((STEPS, 2 * cap, part), bf16),
            pltpu.VMEM((3, 2 * cap, part), bf16),
            pltpu.VMEM((4, 2, cap, part), bf16),
            pltpu.VMEM((4 * cap, part), bf16),
            dma((7,)),
            dma((2,)),
            dma((2,)),
            dma((11,)),
            dma((STEPS, 2)),
            dma((STEPS, 2)),
            dma((STEPS, 2)),
            dma((STEPS, 2)),
            dma((STEPS, 2)),
            dma((STEPS, 2)),
            dma((STEPS, 2)),
            dma((STEPS, 2)),
            dma((STEPS, 2)),
            dma((STEPS, 2)),
            dma((STEPS, 2)),
            dma((STEPS, 2)),
            dma((3, 2)),
            dma((4, 2)),
        ],
        compiler_params=pltpu.CompilerParams(
            collective_id=0, has_side_effects=True, vmem_limit_bytes=60 * 1024 * 1024
        ),
    )(
        tokens[0],
        modality,
        routes.reshape(1, tok),
        norm_gain.reshape(1, width),
        jnp.transpose(router, (0, 2, 1)),
        jnp.transpose(gate_weight[0]),
        down_weight[0],
    )
    return result[None]


def solution(mesh):
    placed = (
        P("pipe", "expert", None),
        P("pipe", "expert"),
        P("pipe", "expert", None),
        P(),
        P(),
        P("pipe", "dp", "expert"),
        P("pipe", "expert", "dp"),
    )
    return jax.shard_map(
        local, mesh=mesh, in_specs=placed, out_specs=P("pipe", "expert", "dp"), check_vma=False
    )
```

time: 129 us -> 128 us (level)
  the two profiles are of different devices: /device:TPU:110 before, /device:TPU:222 now
where the time goes in v3:
time: 128 us; the launch traced here: 127 us
  Pallas kernels  126 us (98%)
  local copies, waits for them, and re-layouts  1.67 us (1%)
    pallas_call x1, Pallas kernels, local(): pl.pallas_call(functools.partial(kernel, n_pipe, n_dp), out_shape=jax.Sha...  126 us

profile of v3, /device:TPU:222, one launch (start us, length us, event | category | flops | bytes accessed | tf_op | source)
XLA Modules:
  0.0 127.3 jit_solution(5586732720187536356)
XLA Ops:
  0.0 125.7 %shard_map.73 = bf16[128,1024]{1,0:T(8,128)(2,1)} custom-call(bf16[128,4096]{1,0:T(8,128)(2,1)} %bitcast.10, s32[1,128]{1,0:T(1,128)} %modality_hbm.1, s32[1,128]{1,0:T(1,128)} %bitcast.15, f32[1,4096]{1,0:T(1,128)} %bitcast.14, bf16[2,4,4096]{2,1,0:T(4,128)(2,1)} %bitcast.13, bf16[448,1024]{1,0:T(8,128)(2,1)} %bitcast.11, bf16[448,1024]{1,0:T(8,128)(2,1)} %bitcast.12), custom_call_target="tpu_custom_call" | custom-call | tf_op jit(solution)/shard_map/pallas_call | solution.py:415
  125.7 1.7 %copy.9 = bf16[1,128,1024]{2,1,0:T(8,128)(2,1)} copy(bf16[1,128,1024]{2,1,0:T(8,128)(2,1)} %bitcast.9) | data formatting | bytes 524288

commit v4 on v3

v4 whole, which is shorter than its diff:
```python
import functools

import jax
import jax.numpy as jnp
from jax import lax
from jax.experimental import pallas as pl
from jax.experimental.pallas import tpu as pltpu
from jax.sharding import PartitionSpec as P

MESH = pl.DeviceIdType.MESH
epsilon = 1e-06
Z = 8
STEPS = 8


def kernel(
    n_pipe, n_dp,
    tokens, modality_hbm, routes_hbm, gain_hbm, router_hbm, gate_hbm, down_hbm,
    out,
    modality, routes, gain, router, tok_v, normed_v, gate_v, down_v, arrived, stat_tx, stat_rx, placer, unplacer, chosen,
    packed, recv, sum_tx, sum_rx, own_sum, hid, term, ret_tx, joint, own_rx, fin, summed,
    local_sem, pipe_send, pipe_recv, first_send, forward_send, dispatch_recv,
    sum_send, sum_recv, hid_send, hid_recv, ret_send, joint_recv, own_recv, fin_recv,
):
    tok = tok_v.shape[0]
    cap = recv.shape[1] // 2
    part = recv.shape[2]
    piece = sum_rx.shape[2]
    s, j, d = lax.axis_index("pipe"), lax.axis_index("expert"), lax.axis_index("dp")
    xl, z = j // Z, j % Z
    g, p = z // 4, z % 4
    mid = ((p + 1) // 2) % 2
    nd = 2 * (p // 2) - 1
    near, far = (z + nd + Z) % Z, (z - nd + Z) % Z
    entry = (z + nd * (1 + mid) + Z) % Z
    other = 1 - xl
    is_mid = mid == 1
    is_end = mid == 0

    def at(x, zz):
        return (s, x * Z + zz, d)

    def send(src, dst, send_sem, recv_sem, device):
        return pltpu.make_async_remote_copy(
            src_ref=src, dst_ref=dst, send_sem=send_sem, recv_sem=recv_sem,
            device_id=device, device_id_type=MESH,
        )

    def rows(ref, zz, x):
        return ref.at[zz, pl.ds(pl.multiple_of(x * cap, cap), cap)]

    tok_copy = pltpu.make_async_copy(tokens, tok_v, local_sem.at[0])
    gate_copy = pltpu.make_async_copy(gate_hbm, gate_v, local_sem.at[1])
    down_copy = pltpu.make_async_copy(down_hbm, down_v, local_sem.at[2])
    small = [
        pltpu.make_async_copy(a, b, local_sem.at[3 + k])
        for k, (a, b) in enumerate(((modality_hbm, modality), (routes_hbm, routes), (gain_hbm, gain), (router_hbm, router)))
    ]
    for copy in small:
        copy.start()
    tok_copy.start()

    barrier = pltpu.get_barrier_semaphore()
    partners = [
        ((s + 1) % n_pipe, j, d),
        ((s + n_pipe - 1) % n_pipe, j, d),
        at(other, z), at(xl, far),
    ] + [(s, j, (d + k) % n_dp) for k in range(1, n_dp)]
    for steps in (1 + 2 * mid, 2):
        partners += [at(x, (z + nd * steps + Z) % Z) for x in (xl, other)]
    for device in partners:
        pl.semaphore_signal(barrier, inc=1, device_id=device, device_id_type=MESH)

    @pl.when(is_mid)
    def _():
        pl.semaphore_signal(barrier, inc=1, device_id=at(xl, near), device_id_type=MESH)

    gate_copy.start()
    down_copy.start()
    for copy in small:
        copy.wait()

    route_row = routes[...]
    hits = (lax.broadcasted_iota(jnp.int32, (8, tok), 0) == route_row).astype(jnp.float32)
    before = (
        lax.broadcasted_iota(jnp.int32, (tok, tok), 0) < lax.broadcasted_iota(jnp.int32, (tok, tok), 1)
    ).astype(jnp.bfloat16)
    earlier = jnp.dot(hits.astype(jnp.bfloat16), before, preferred_element_type=jnp.float32)
    rank = jnp.sum(hits * earlier, axis=0, keepdims=True)
    slot_row = route_row.astype(jnp.float32) * cap + rank
    slots = lax.broadcasted_iota(jnp.int32, (4 * cap, tok), 0).astype(jnp.float32)
    placer[...] = (slots == slot_row).astype(jnp.bfloat16)
    slot_col = jnp.transpose(jnp.broadcast_to(slot_row, (tok, tok)))[:, 0:1]
    slots = lax.broadcasted_iota(jnp.int32, (tok, 4 * cap), 1).astype(jnp.float32)
    unplacer[...] = (slots == slot_col).astype(jnp.bfloat16)
    pick_row = (modality[...] * 4 + route_row).astype(jnp.float32)
    pick_col = jnp.transpose(jnp.broadcast_to(pick_row, (tok, tok)))[:, 0:1]
    lanes = lax.broadcasted_iota(jnp.int32, (tok, 128), 1).astype(jnp.float32)
    chosen[...] = (lanes == pick_col).astype(jnp.float32)

    pl.semaphore_wait(barrier, len(partners) + mid)

    following = ((s + 1) % n_pipe, j, d)
    own_columns = pl.ds(pl.multiple_of(d * part, part), part)
    raw_copy = send(tokens.at[:, own_columns], arrived, pipe_send.at[0], pipe_recv.at[0], following)
    raw_copy.start()

    stat_tx[...] = jnp.zeros_like(stat_tx)
    tok_copy.wait()

    def norm_rows(i, carry):
        block = pl.ds(pl.multiple_of(i * 16, 16), 16)
        x = tok_v[block, :].astype(jnp.float32)
        scale = lax.rsqrt(jnp.mean(x * x, axis=-1, keepdims=True) + epsilon)
        normed_v[block, :] = (x * scale * gain[...]).astype(jnp.bfloat16)
        stat_tx[block, 8:9] = scale
        return carry

    lax.fori_loop(0, tok // 16, norm_rows, 0)
    for kind in range(2):
        stat_tx[:, 4 * kind : 4 * kind + 4] = lax.dot_general(
            normed_v[...], router[kind], (((1,), (1,)), ((), ())), preferred_element_type=jnp.float32
        )
    stat_copy = send(stat_tx, stat_rx, pipe_send.at[1], pipe_recv.at[1], following)
    stat_copy.start()
    raw_copy.wait_recv()
    stat_copy.wait_recv()

    scale = stat_rx[:, 8:9]
    normed = (arrived[...].astype(jnp.float32) * scale * gain[:, own_columns]).astype(jnp.bfloat16)

    def pack(x, group):
        spot = pl.ds(pl.multiple_of((2 * x + group) * cap, cap), cap)
        return jnp.dot(placer[spot, :], normed, preferred_element_type=jnp.float32).astype(jnp.bfloat16)

    packed[0] = pack(other, g)
    cross = send(packed.at[0], rows(recv, z, xl), first_send.at[0], dispatch_recv.at[z, xl], at(other, z))
    cross.start()
    packed[1] = pack(xl, 1 - g)
    ext_own = send(packed.at[1], rows(recv, z, xl), first_send.at[1], dispatch_recv.at[z, xl], at(xl, entry))
    ext_own.start()
    recv[z, pl.ds(pl.multiple_of(xl * cap, cap), cap), :] = pack(xl, g)

    def inside(x, first):
        block = rows(recv, z, x)
        return [
            send(block, block, first_send.at[first + k], dispatch_recv.at[z, x], at(xl, target))
            for k, target in enumerate((far, near))
        ]

    own_sends, relay_sends = inside(xl, 3), inside(other, 5)

    def start_inside(copies):
        copies[0].start()

        @pl.when(is_mid)
        def _():
            copies[1].start()

    start_inside(own_sends)
    packed[2] = pack(other, 1 - g)
    ext_other = send(packed.at[2], rows(recv, z, xl), first_send.at[2], dispatch_recv.at[z, xl], at(other, entry))
    ext_other.start()
    relay_sends[0].wait_recv()
    start_inside(relay_sends)

    gate_copy.wait()
    down_copy.wait()

    def source(t):
        at_mid = (t % 2) * ((t + 1) // 2) - (1 - t % 2) * (t // 2)
        at_end = sum(
            offset * (1 - ((t - k) * (t - k) + 48) // 49) for k, offset in enumerate((0, -1, 1, -2, -3, 2, -4, -5))
        )
        return (z + nd * (mid * at_mid + (1 - mid) * at_end) + 2 * Z) % Z

    def passed_on(t):
        return (z + nd * ((t + 1) // 2) + Z) % Z

    def forward(t, zz, x):
        to_near = mid * (1 - (t % 2) * (1 - t // 7))
        target = (z + nd * (2 * to_near - 1) + Z) % Z
        return send(rows(recv, zz, x), rows(recv, zz, x), forward_send.at[t, x], dispatch_recv.at[zz, x], at(xl, target))

    def end_forwards(t):
        return is_end & ((t == 1) | (t == 3))

    def span(ref, t, q):
        return ref.at[t, pl.ds(pl.multiple_of(q * piece, piece), piece)]

    def sum_copy(t, k):
        q = (d + k) % n_dp
        return send(span(sum_tx, t, q), sum_rx.at[t, k - 1], sum_send.at[t, k - 1], sum_recv.at[t, k - 1], (s, j, q))

    def hid_copy(t, k):
        own = span(hid, t, d)
        return send(own, own, hid_send.at[t, k - 1], hid_recv.at[t, k - 1], (s, j, (d + k) % n_dp))

    own_expert = 2 * xl + g

    def joint_copy(zz, x, target):
        return send(rows(ret_tx, zz, x), rows(joint, zz, x), ret_send.at[zz, x], joint_recv.at[zz, x], at(xl, target))

    def root_copy(zz, x, place, target):
        return send(rows(ret_tx, zz, x), rows(own_rx, place, x), ret_send.at[zz, x], own_recv.at[place, x], at(xl, target))

    def home_copy(zz, x, place):
        return send(rows(ret_tx, zz, x), fin.at[own_expert, place], ret_send.at[zz, x], fin_recv.at[own_expert, place], at(x, zz))

    def each_step(i, carry):
        @pl.when(i <= 7)
        def _():
            @pl.when(end_forwards(i))
            def _():
                for x in (xl, other):
                    forward(i, passed_on(i), x).wait_recv()
                    forward(i, passed_on(i), x).start()

            zz = source(i)
            for x in (xl, other):
                @pl.when((i >= 1) & (is_mid | ((i != 2) & (i != 5))))
                def _():
                    forward(i, zz, x).wait_recv()

                @pl.when((i >= 1) & is_mid)
                def _():
                    forward(i, zz, x).start()

            terms = lax.dot_general(
                gate_v[...], recv[zz], (((1,), (1,)), ((), ())), preferred_element_type=jnp.float32
            )
            own_sum[i % 4] = terms
            sum_tx[i] = terms.astype(jnp.bfloat16)
            for k in range(1, n_dp):
                sum_copy(i, k).start()

        @pl.when((i >= 1) & (i <= 8))
        def _():
            t = i - 1
            mine = pl.ds(pl.multiple_of(d * piece, piece), piece)
            total = own_sum[t % 4, mine, :]
            for k in range(1, n_dp):
                sum_copy(t, k).wait_recv()
                total = total + sum_rx[t, k - 1].astype(jnp.float32)
            hid[t, mine, :] = (total / (1.0 + jnp.exp(-total))).astype(jnp.bfloat16)
            for k in range(1, n_dp):
                hid_copy(t, k).start()

        @pl.when((i >= 2) & (i <= 9))
        def _():
            t = i - 2
            zz = source(t)
            for k in range(1, n_dp):
                hid_copy(t, k).wait_recv()
            term[zz] = lax.dot_general(
                hid[t], down_v[...], (((0,), (0,)), ((), ())), preferred_element_type=jnp.float32
            )

            @pl.when(is_end & (t >= 1))
            def _():
                ret_tx[zz] = term[zz].astype(jnp.bfloat16)

            for x in range(2):
                @pl.when(is_end & ((t == 2) | (t == 5)))
                def _():
                    home_copy(zz, x, 0).start()

                @pl.when(is_end & (t == 1))
                def _():
                    root_copy(zz, x, 0, far).start()

                @pl.when(is_end & ((t == 3) | (t == 4) | (t >= 6)))
                def _():
                    joint_copy(zz, x, far).start()

        def join(zz, x):
            block = slice(x * cap, (x + 1) * cap)
            joint_copy(zz, x, far).wait_recv()
            ret_tx[zz, block] = (term[zz, block] + joint[zz, block].astype(jnp.float32)).astype(jnp.bfloat16)

        @pl.when(is_mid & (i >= 6) & (i <= 10) & (i != 8))
        def _():
            u = i - 6
            zz = (z + nd * (u // 3 - u - 1) + Z) % Z
            for x in range(2):
                join(zz, x)

                @pl.when(i == 6)
                def _():
                    root_copy(zz, x, 1, far).start()

                @pl.when(i >= 7)
                def _():
                    joint_copy(zz, x, far).start()

        @pl.when(is_mid & ((i == 8) | (i >= 10)))
        def _():
            v = i - 8
            zz = (z + nd * (1 + v - v // 2) + Z) % Z
            for x in range(2):
                join(zz, x)

                @pl.when(i == 8)
                def _():
                    root_copy(zz, x, 1, near).start()

                @pl.when(i >= 10)
                def _():
                    home_copy(zz, x, 1).start()

        @pl.when(i == 9 - mid)
        def _():
            for x in (other, xl):
                block = pl.ds(pl.multiple_of(x * cap, cap), cap)
                root_copy(z, x, 1, far).wait_recv()
                total = term[z, block, :] + own_rx[1, block, :].astype(jnp.float32)

                @pl.when(is_end)
                def _():
                    ret_tx[z, block, :] = total.astype(jnp.bfloat16)

                @pl.when(is_mid)
                def _():
                    root_copy(z, x, 0, near).wait_recv()
                    ret_tx[z, block, :] = (total + own_rx[0, block, :].astype(jnp.float32)).astype(jnp.bfloat16)

                if x is other:
                    home_copy(z, other, 0).start()

        return carry

    lax.fori_loop(0, 12, each_step, 0)

    summed[pl.ds(pl.multiple_of(own_expert * cap, cap), cap), :] = ret_tx[z, pl.ds(pl.multiple_of(xl * cap, cap), cap), :]

    def arrival(e, place):
        return send(fin.at[e, place], fin.at[e, place], ret_send.at[0, 0], fin_recv.at[e, place], at(other, z))

    for x in (xl, other):
        e = 2 * x + 1 - g
        for place in range(2):
            arrival(e, place).wait_recv()
        summed[pl.ds(pl.multiple_of(e * cap, cap), cap), :] = (
            fin[e, 0].astype(jnp.float32) + fin[e, 1].astype(jnp.float32)
        ).astype(jnp.bfloat16)
    e = 2 * other + g
    arrival(e, 0).wait_recv()
    summed[pl.ds(pl.multiple_of(e * cap, cap), cap), :] = fin[e, 0]

    gate_value = 1.0 / (1.0 + jnp.exp(-jnp.sum(chosen[...] * stat_rx[...], axis=1, keepdims=True)))
    expert_out = jnp.dot(
        unplacer[...], summed[...], preferred_element_type=jnp.float32
    )
    out[...] = (arrived[...].astype(jnp.float32) + gate_value * expert_out).astype(jnp.bfloat16)

    raw_copy.wait_send()
    stat_copy.wait_send()
    for copy in (cross, ext_own, ext_other, own_sends[0], relay_sends[0]):
        copy.wait_send()

    @pl.when(is_mid)
    def _():
        own_sends[1].wait_send()
        relay_sends[1].wait_send()

    def sent(t, carry):
        zz = source(t)

        @pl.when(end_forwards(t) | ((t >= 1) & is_mid))
        def _():
            for x in range(2):
                forward(t, zz, x).wait_send()

        for k in range(1, n_dp):
            sum_copy(t, k).wait_send()
            hid_copy(t, k).wait_send()

        @pl.when(t >= 1)
        def _():
            for x in range(2):
                joint_copy(zz, x, far).wait_send()

        return carry

    lax.fori_loop(0, STEPS, sent, 0)
    home_copy(z, other, 0).wait_send()


def local(tokens, modality, routes, norm_gain, router, gate_weight, down_weight):
    tok, width = tokens.shape[1:]
    n_pipe, n_dp = lax.axis_size("pipe"), lax.axis_size("dp")
    part = width // n_dp
    cap = 2 * tok // router.shape[2]
    hidden = gate_weight.shape[2]
    piece = hidden // n_dp
    bf16, f32 = jnp.bfloat16, jnp.float32
    vmem = pl.BlockSpec(memory_space=pltpu.VMEM)
    anywhere = pl.BlockSpec(memory_space=pl.ANY)
    dma = pltpu.SemaphoreType.DMA
    result = pl.pallas_call(
        functools.partial(kernel, n_pipe, n_dp),
        out_shape=jax.ShapeDtypeStruct((tok, part), bf16),
        in_specs=[anywhere] * 7,
        out_specs=vmem,
        scratch_shapes=[
            pltpu.VMEM((1, tok), jnp.int32),
            pltpu.VMEM((1, tok), jnp.int32),
            pltpu.VMEM((1, width), f32),
            pltpu.VMEM((router.shape[0], router.shape[2], width), bf16),
            pltpu.VMEM((tok, width), bf16),
            pltpu.VMEM((tok, width), bf16),
            pltpu.VMEM((hidden, part), bf16),
            pltpu.VMEM((hidden, part), bf16),
            pltpu.VMEM((tok, part), bf16),
            pltpu.VMEM((tok, 128), f32),
            pltpu.VMEM((tok, 128), f32),
            pltpu.VMEM((4 * cap, tok), bf16),
            pltpu.VMEM((tok, 4 * cap), bf16),
            pltpu.VMEM((tok, 128), f32),
            pltpu.VMEM((3, cap, part), bf16),
            pltpu.VMEM((STEPS, 2 * cap, part), bf16),
            pltpu.VMEM((STEPS, hidden, 2 * cap), bf16),
            pltpu.VMEM((STEPS, n_dp - 1, piece, 2 * cap), bf16),
            pltpu.VMEM((4, hidden, 2 * cap), f32),
            pltpu.VMEM((STEPS, hidden, 2 * cap), bf16),
            pltpu.VMEM((STEPS, 2 * cap, part), f32),
            pltpu.VMEM((STEPS, 2 * cap, part), bf16),
            pltpu.VMEM((STEPS, 2 * cap, part), bf16),
            pltpu.VMEM((2, 2 * cap, part), bf16),
            pltpu.VMEM((4, 2, cap, part), bf16),
            pltpu.VMEM((4 * cap, part), bf16),
            dma((7,)),
            dma((2,)),
            dma((2,)),
            dma((7,)),
            dma((STEPS, 2)),
            dma((STEPS, 2)),
            dma((STEPS, n_dp - 1)),
            dma((STEPS, n_dp - 1)),
            dma((STEPS, n_dp - 1)),
            dma((STEPS, n_dp - 1)),
            dma((STEPS, 2)),
            dma((STEPS, 2)),
            dma((2, 2)),
            dma((4, 2)),
        ],
        compiler_params=pltpu.CompilerParams(
            collective_id=0, has_side_effects=True, vmem_limit_bytes=60 * 1024 * 1024
        ),
    )(
        tokens[0],
        modality,
        routes.reshape(1, tok),
        norm_gain.reshape(1, width),
        jnp.transpose(router, (0, 2, 1)),
        jnp.transpose(gate_weight[0]),
        down_weight[0],
    )
    return result[None]


def solution(mesh):
    placed = (
        P("pipe", "expert", None),
        P("pipe", "expert"),
        P("pipe", "expert", None),
        P(),
        P(),
        P("pipe", "dp", "expert"),
        P("pipe", "expert", "dp"),
    )
    return jax.shard_map(
        local, mesh=mesh, in_specs=placed, out_specs=P("pipe", "expert", "dp"), check_vma=False
    )
```

time: 128 us -> 111 us (0.87)
  the two profiles are of different devices: /device:TPU:222 before, /device:TPU:12 now
where the time goes in v4:
time: 111 us; the launch traced here: 110 us
  Pallas kernels  109 us (98%)
  local copies, waits for them, and re-layouts  1.67 us (2%)
    pallas_call x1, Pallas kernels, local(): pl.pallas_call(functools.partial(kernel, n_pipe, n_dp), out_shape=jax.Sha...  109 us

profile of v4, /device:TPU:12, one launch (start us, length us, event | category | flops | bytes accessed | tf_op | source)
XLA Modules:
  0.0 110.4 jit_solution(7420216032519096923)
XLA Ops:
  0.0 108.7 %shard_map.73 = bf16[128,1024]{1,0:T(8,128)(2,1)} custom-call(bf16[128,4096]{1,0:T(8,128)(2,1)} %bitcast.10, s32[1,128]{1,0:T(1,128)} %modality_hbm.1, s32[1,128]{1,0:T(1,128)} %bitcast.15, f32[1,4096]{1,0:T(1,128)} %bitcast.14, bf16[2,4,4096]{2,1,0:T(4,128)(2,1)} %bitcast.13, bf16[448,1024]{1,0:T(8,128)(2,1)} %bitcast.11, bf16[448,1024]{1,0:T(8,128)(2,1)} %bitcast.12), custom_call_target="tpu_custom_call" | custom-call | tf_op jit(solution)/shard_map/pallas_call | solution.py:400
  108.7 1.7 %copy.9 = bf16[1,128,1024]{2,1,0:T(8,128)(2,1)} copy(bf16[1,128,1024]{2,1,0:T(8,128)(2,1)} %bitcast.9) | data formatting | bytes 524288

commit v5 on v4

--- a/solution.py
+++ b/solution.py
@@ -139,6 +139,9 @@
     packed[1] = pack(xl, 1 - g)
     ext_own = send(packed.at[1], rows(recv, z, xl), first_send.at[1], dispatch_recv.at[z, xl], at(xl, entry))
     ext_own.start()
+    packed[2] = pack(other, 1 - g)
+    ext_other = send(packed.at[2], rows(recv, z, xl), first_send.at[2], dispatch_recv.at[z, xl], at(other, entry))
+    ext_other.start()
     recv[z, pl.ds(pl.multiple_of(xl * cap, cap), cap), :] = pack(xl, g)
 
     def inside(x, first):
@@ -158,9 +161,6 @@
             copies[1].start()
 
     start_inside(own_sends)
-    packed[2] = pack(other, 1 - g)
-    ext_other = send(packed.at[2], rows(recv, z, xl), first_send.at[2], dispatch_recv.at[z, xl], at(other, entry))
-    ext_other.start()
     relay_sends[0].wait_recv()
     start_inside(relay_sends)
 
@@ -218,13 +218,9 @@
 
             zz = source(i)
             for x in (xl, other):
-                @pl.when((i >= 1) & (is_mid | ((i != 2) & (i != 5))))
+                @pl.when(is_end & (i >= 1) & (i != 2) & (i != 5))
                 def _():
                     forward(i, zz, x).wait_recv()
-
-                @pl.when((i >= 1) & is_mid)
-                def _():
-                    forward(i, zz, x).start()
 
             terms = lax.dot_general(
                 gate_v[...], recv[zz], (((1,), (1,)), ((), ())), preferred_element_type=jnp.float32
@@ -246,6 +242,12 @@
             for k in range(1, n_dp):
                 hid_copy(t, k).start()
 
+        @pl.when(is_mid & (i <= 6))
+        def _():
+            zz = source(i + 1)
+            forward(i + 1, zz, xl).wait_recv()
+            forward(i + 1, zz, xl).start()
+
         @pl.when((i >= 2) & (i <= 9))
         def _():
             t = i - 2
@@ -272,6 +274,12 @@
                 @pl.when(is_end & ((t == 3) | (t == 4) | (t >= 6)))
                 def _():
                     joint_copy(zz, x, far).start()
+
+        @pl.when(is_mid & (i <= 6))
+        def _():
+            zz = source(i + 1)
+            forward(i + 1, zz, other).wait_recv()
+            forward(i + 1, zz, other).start()
 
         def join(zz, x):
             block = slice(x * cap, (x + 1) * cap)

time: 111 us -> 108 us (0.973)
  the two profiles are of different devices: /device:TPU:12 before, /device:TPU:209 now
where the time goes in v5:
time: 108 us
  Pallas kernels  106 us (98%)
  local copies, waits for them, and re-layouts  1.67 us (2%)
    pallas_call x1, Pallas kernels, local(): pl.pallas_call(functools.partial(kernel, n_pipe, n_dp), out_shape=jax.Sha...  106 us

profile of v5, /device:TPU:209, one launch (start us, length us, event | category | flops | bytes accessed | tf_op | source)
XLA Modules:
  0.0 108.0 jit_solution(18120996270336503745)
XLA Ops:
  0.0 106.3 %shard_map.73 = bf16[128,1024]{1,0:T(8,128)(2,1)} custom-call(bf16[128,4096]{1,0:T(8,128)(2,1)} %bitcast.10, s32[1,128]{1,0:T(1,128)} %modality_hbm.1, s32[1,128]{1,0:T(1,128)} %bitcast.15, f32[1,4096]{1,0:T(1,128)} %bitcast.14, bf16[2,4,4096]{2,1,0:T(4,128)(2,1)} %bitcast.13, bf16[448,1024]{1,0:T(8,128)(2,1)} %bitcast.11, bf16[448,1024]{1,0:T(8,128)(2,1)} %bitcast.12), custom_call_target="tpu_custom_call" | custom-call | tf_op jit(solution)/shard_map/pallas_call | solution.py:408
  106.3 1.7 %copy.9 = bf16[1,128,1024]{2,1,0:T(8,128)(2,1)} copy(bf16[1,128,1024]{2,1,0:T(8,128)(2,1)} %bitcast.9) | data formatting | bytes 524288

commit v6 on v5

--- a/solution.py
+++ b/solution.py
@@ -339,6 +339,33 @@
 
     lax.fori_loop(0, 12, each_step, 0)
 
+    raw_copy.wait_send()
+    stat_copy.wait_send()
+    for copy in (cross, ext_own, ext_other, own_sends[0], relay_sends[0]):
+        copy.wait_send()
+
+    @pl.when(is_mid)
+    def _():
+        own_sends[1].wait_send()
+        relay_sends[1].wait_send()
+
+    def sent(t, carry):
+        zz = source(t)
+
+        @pl.when(end_forwards(t) | ((t >= 1) & is_mid))
+        def _():
+            for x in range(2):
+                forward(t, zz, x).wait_send()
+
+        for k in range(1, n_dp):
+            sum_copy(t, k).wait_send()
+            hid_copy(t, k).wait_send()
+
+        return carry
+
+    lax.fori_loop(0, STEPS, sent, 0)
+
+    gate_value = 1.0 / (1.0 + jnp.exp(-jnp.sum(chosen[...] * stat_rx[...], axis=1, keepdims=True)))
     summed[pl.ds(pl.multiple_of(own_expert * cap, cap), cap), :] = ret_tx[z, pl.ds(pl.multiple_of(xl * cap, cap), cap), :]
 
     def arrival(e, place):
@@ -355,42 +382,17 @@
     arrival(e, 0).wait_recv()
     summed[pl.ds(pl.multiple_of(e * cap, cap), cap), :] = fin[e, 0]
 
-    gate_value = 1.0 / (1.0 + jnp.exp(-jnp.sum(chosen[...] * stat_rx[...], axis=1, keepdims=True)))
     expert_out = jnp.dot(
         unplacer[...], summed[...], preferred_element_type=jnp.float32
     )
     out[...] = (arrived[...].astype(jnp.float32) + gate_value * expert_out).astype(jnp.bfloat16)
 
-    raw_copy.wait_send()
-    stat_copy.wait_send()
-    for copy in (cross, ext_own, ext_other, own_sends[0], relay_sends[0]):
-        copy.wait_send()
-
-    @pl.when(is_mid)
-    def _():
-        own_sends[1].wait_send()
-        relay_sends[1].wait_send()
-
-    def sent(t, carry):
-        zz = source(t)
-
-        @pl.when(end_forwards(t) | ((t >= 1) & is_mid))
-        def _():
-            for x in range(2):
-                forward(t, zz, x).wait_send()
-
-        for k in range(1, n_dp):
-            sum_copy(t, k).wait_send()
-            hid_copy(t, k).wait_send()
-
-        @pl.when(t >= 1)
-        def _():
-            for x in range(2):
-                joint_copy(zz, x, far).wait_send()
-
+    def returned(t, carry):
+        for x in range(2):
+            joint_copy(source(t), x, far).wait_send()
         return carry
 
-    lax.fori_loop(0, STEPS, sent, 0)
+    lax.fori_loop(1, STEPS, returned, 0)
     home_copy(z, other, 0).wait_send()
 
 

time: 108 us -> 108 us (level)
  no operation moved by 1% of the time
where the time goes in v6:
time: 108 us
  Pallas kernels  106 us (98%)
  local copies, waits for them, and re-layouts  1.67 us (2%)
    pallas_call x1, Pallas kernels, local(): pl.pallas_call(functools.partial(kernel, n_pipe, n_dp), out_shape=jax.Sha...  106 us

profile of v6, /device:TPU:209, one launch (start us, length us, event | category | flops | bytes accessed | tf_op | source)
XLA Modules:
  0.0 107.7 jit_solution(16011292757573453858)
XLA Ops:
  0.0 106.0 %shard_map.73 = bf16[128,1024]{1,0:T(8,128)(2,1)} custom-call(bf16[128,4096]{1,0:T(8,128)(2,1)} %bitcast.10, s32[1,128]{1,0:T(1,128)} %modality_hbm.1, s32[1,128]{1,0:T(1,128)} %bitcast.15, f32[1,4096]{1,0:T(1,128)} %bitcast.14, bf16[2,4,4096]{2,1,0:T(4,128)(2,1)} %bitcast.13, bf16[448,1024]{1,0:T(8,128)(2,1)} %bitcast.11, bf16[448,1024]{1,0:T(8,128)(2,1)} %bitcast.12), custom_call_target="tpu_custom_call" | custom-call | tf_op jit(solution)/shard_map/pallas_call | solution.py:410
  106.0 1.7 %copy.9 = bf16[1,128,1024]{2,1,0:T(8,128)(2,1)} copy(bf16[1,128,1024]{2,1,0:T(8,128)(2,1)} %bitcast.9) | data formatting | bytes 524288
